TPU v7x, 32 devices: a whole 2x2x4 slice. The times are simulated.
32 devices in a mesh: group: 4 (over y, core), dev: 8 (over z, x).
Axes of the slice: x: 2, y: 2, z: 4, core: 2. Of those that a mesh axis runs over, the one named last changes fastest.
Arguments:
- primary_q: bfloat16 [64, 3584, 1024], P(('group', 'dev')), may hold values from -0.09375 to 0.09375
- primary_scales: bfloat16 [64, 28, 8], P(('group', 'dev')), may hold values from 0.5 to 2
- new_place: int32 [32], P(('group', 'dev')), may hold values from 0 to 63, as said below
- tokens: bfloat16 [512, 3584], P(('group', 'dev')), may hold values from -6 to 6
- experts: int32 [512, 8], P(('group', 'dev')), may hold values from 0 to 63, all different within a row
- replica: int32 [512, 8], P(('group', 'dev')), may hold values from 0 to 1
- route_num: int32 [512, 8], P(('group', 'dev')), may hold values from 1 to 16
Outputs:
- new_weights: bfloat16 [32, 3584, 1024], P(('group', 'dev'))
- new_scales: bfloat16 [32, 28, 8], P(('group', 'dev'))
- hidden_out: bfloat16 [512, 8, 1024], P(('group', 'dev'))
- slot_load: int32 [32, 3], P(('group', 'dev'))
Inputs may be any that keep to these rules, and one draw needn't show every extreme that they name: `new_place`: the redundant slots of the 8 devices of one group hold 8 different experts, each with its primary copy on a device of that group.
All inputs are finite; a program needn't handle non-finite values.
Results may differ from a plain program's by a relative error of at most 0.0057.
Values may be sent and summed in bfloat16 or wider, within the bound.
No kernel may reach another device: no remote copies, remote signals or barrier semaphores. Data moves between devices by JAX's collectives and lax.ppermute only.
A program may use at most 192 MiB of HBM per device.

v0:
```python
import jax
import jax.numpy as jnp
from jax import lax
from jax.sharding import PartitionSpec as P

D = 3584
FF = 1024
TILE = 128
CAP = 2


def dequantize(values, scales):
    tile_grid = values.astype(jnp.float32).reshape(D // TILE, TILE, FF // TILE, TILE)
    scaled = tile_grid * scales.astype(jnp.float32)[:, None, :, None]
    return scaled.reshape(D, FF).astype(jnp.bfloat16)


def spread_parts(values, scales, parts_count):
    holding, width_in, hidden = values.shape
    split_values = values.reshape(holding, parts_count, width_in // parts_count, hidden)
    split_scales = jnp.broadcast_to(scales[:, None], (holding, parts_count) + scales.shape[1:])
    return (split_values, split_scales)


def pick_parts(got_values, got_scales, wanted, first_dev):
    holding = got_values.shape[0]
    parts_count = got_values.shape[1]
    chosen = wanted % holding * parts_count + (wanted // holding - first_dev)
    values = got_values.reshape((holding * parts_count,) + got_values.shape[2:])[chosen]
    scales = got_scales.reshape((holding * parts_count,) + got_scales.shape[2:])[chosen]
    return (values, scales)


def per_device(primary_q, primary_scales, new_place, tokens, experts, replica, route_num):
    place_all = lax.all_gather(new_place, ("group", "dev"), axis=0, tiled=True)
    holding = primary_q.shape[0]
    parts_count = lax.axis_size("dev")
    first_dev = lax.axis_index("group") * parts_count
    wanted = lax.dynamic_slice_in_dim(place_all, first_dev, parts_count)
    split_values, split_scales = spread_parts(primary_q, primary_scales, parts_count)
    got_values, got_scales = (
        lax.all_to_all(split_values, "dev", split_axis=1, concat_axis=1, tiled=True),
        lax.all_to_all(split_scales, "dev", split_axis=1, concat_axis=1, tiled=True),
    )
    send_values, send_scales = pick_parts(got_values, got_scales, wanted, first_dev)
    back_values, back_scales = (
        lax.all_to_all(send_values, "dev", split_axis=0, concat_axis=0, tiled=True),
        lax.all_to_all(send_scales, "dev", split_axis=0, concat_axis=0, tiled=True),
    )
    new_weights = back_values.reshape((1, D, FF))
    new_scales = back_scales[0:1]
    row_count, top_count = experts.shape
    pair_count = row_count * top_count
    device_count = place_all.shape[0]
    expert_flat = experts.reshape(pair_count)
    device_ids = jnp.arange(device_count, dtype=jnp.int32)
    matched = expert_flat[:, None] == place_all[None, :]
    has_copy = jnp.any(matched, axis=1)
    holder = jnp.sum(jnp.where(matched, device_ids[None, :], 0), axis=1)
    use_copy = (replica.reshape(pair_count) == 1) & has_copy
    target = jnp.where(use_copy, holder, expert_flat // holding)
    slot_id = jnp.where(use_copy, holding, expert_flat % holding)
    pair_order = jnp.arange(pair_count)
    earlier = (target[:, None] == target[None, :]) & (pair_order[None, :] < pair_order[:, None])
    position = jnp.sum(earlier, axis=1)
    served = position < CAP
    cell_count = device_count * CAP
    cell_index = target * CAP + position
    placed = (cell_index[None, :] == jnp.arange(cell_count)[:, None]) & served[None, :]
    row_hits = jnp.any(placed.reshape(cell_count, row_count, top_count), axis=2)
    row_buffer = jnp.dot(row_hits.astype(jnp.bfloat16), tokens, preferred_element_type=jnp.float32)
    row_buffer = row_buffer.astype(jnp.bfloat16).reshape(device_count, CAP, D)
    code_values = jnp.sum(jnp.where(placed, slot_id[None, :] + 1, 0), axis=1) - 1
    code_buffer = code_values.astype(jnp.float32).astype(jnp.bfloat16).reshape(device_count, CAP)
    matrices = [dequantize(primary_q[member], primary_scales[member]) for member in range(holding)]
    matrices.append(dequantize(new_weights[0], new_scales[0]))
    joined = jnp.concatenate(matrices, axis=1)
    row_block = lax.all_to_all(
        row_buffer, ("group", "dev"), split_axis=0, concat_axis=0, tiled=True
    )
    slot_codes = lax.all_to_all(
        code_buffer, ("group", "dev"), split_axis=0, concat_axis=0, tiled=True
    )
    leading, item_count, width_in = row_block.shape
    product = jnp.dot(
        row_block.reshape(leading * item_count, width_in),
        joined,
        preferred_element_type=jnp.float32,
    )
    flat_codes = slot_codes.reshape(leading * item_count).astype(jnp.float32)
    picked = jnp.zeros((leading * item_count, FF), jnp.float32)
    tallies = []
    for member in range(holding + 1):
        chosen = flat_codes == member
        picked = picked + jnp.where(
            chosen[:, None], product[:, member * FF : (member + 1) * FF], 0.0
        )
        tallies.append(chosen.astype(jnp.float32))
    activated = jax.nn.silu(picked).astype(jnp.bfloat16).reshape(leading, item_count, FF)
    activated, tallies = (
        activated,
        jnp.stack(tallies, axis=1).reshape(leading, item_count, holding + 1),
    )
    returned = lax.all_to_all(activated, ("group", "dev"), split_axis=0, concat_axis=0, tiled=True)
    dest_hit = (target[None, :] == device_ids[:, None]) & served[None, :]
    slot_hit = slot_id[:, None] == jnp.arange(holding + 1)[None, :]
    counted = jnp.dot(
        dest_hit.astype(jnp.float32), slot_hit.astype(jnp.float32), precision=lax.Precision.HIGHEST
    )
    summed = lax.psum_scatter(counted, ("group", "dev"), scatter_dimension=0, tiled=True)
    slot_load = summed.astype(jnp.int32)
    selected = jnp.dot(
        placed.T.astype(jnp.bfloat16),
        returned.reshape(cell_count, FF),
        preferred_element_type=jnp.float32,
    )
    weight = route_num.reshape(pair_count).astype(jnp.float32) / 16.0
    hidden_out = (selected * weight[:, None]).astype(jnp.bfloat16).reshape(row_count, top_count, FF)
    return (new_weights, new_scales, hidden_out, slot_load)


def solution(mesh):
    in_specs = (
        P(("group", "dev"), None, None),
        P(("group", "dev"), None, None),
        P(("group", "dev")),
        P(("group", "dev"), None),
        P(("group", "dev"), None),
        P(("group", "dev"), None),
        P(("group", "dev"), None),
    )
    out_specs = (
        P(("group", "dev"), None, None),
        P(("group", "dev"), None, None),
        P(("group", "dev"), None, None),
        P(("group", "dev"), None),
    )
    return jax.shard_map(
        per_device, mesh=mesh, in_specs=in_specs, out_specs=out_specs, check_vma=False
    )
```

profile of v0, /device:TPU:0, one launch (start us, length us, event | category | flops | bytes accessed | tf_op | source)
XLA Modules:
  0.0 671.3 jit_solution(3730268365096113086)
XLA Ops:
  1.3 0.7 broadcast_bitcast_fusion
  2.0 0.7 reshape.356
  2.7 0.1 dynamic-update-slice
  2.8 7.3 %all-to-all-start.2 = ((bf16[8,2,224]{2,1,0:T(2,128)(2,1)}), bf16[8,2,224]{2,1,0:T(2,128)(2,1)S(1)}, u32[]{:S(2)}, u32[]{:S(2)}) async-start(bf16[8,2,224]{2,1,0:T(2,128)(2,1)} %reshape.356), calls=%async_computation.2 | async-start | bytes 16384 | tf_op jit(solution)/shard_map/all_to_all | solution.py:43
  10.1 40.8 %all-reduce = s32[32]{0:T(128)S(1)} all-reduce(s32[32]{0:T(128)S(1)} %dynamic-update-slice), channel_id=1, replica_groups=mesh['group'=4,'dev'=8] {'group','dev'}, use_global_device_ids=true, to_apply=%add | all-reduce | flops 32 | bytes 256
  50.9 0.8 copy.62
  51.9 0.8 copy.61
  52.7 0.1 eq.148
  52.8 0.2 convert_reduce_fusion
  53.1 0.1 select_reduce_fusion
  53.2 0.7 convert_element_type.161
  54.0 4.4 all-to-all-start.4
  58.4 0.1 reshape.357
  58.5 1.2 gather_fusion.1
  59.7 5.8 all-to-all-done.4
  65.4 3.3 all-to-all-start.3
  68.8 13.5 %copy.58 = bf16[2,8,448,1024]{3,2,0,1:T(8,128)(2,1)} copy(bf16[2,8,448,1024]{3,2,1,0:T(8,128)(2,1)} %bitcast.49) | data formatting | bytes 29360128 | tf_op jit(solution)/shard_map/reshape | solution.py:20
  82.2 5.9 all-to-all-start
  88.3 0.1 reduce_or.21
  88.5 0.1 fusion.15
  88.6 0.3 convolution_convert_fusion
  88.9 1.0 reshape.322
  89.9 316.1 %all-to-all-done = bf16[2,8,448,1024]{3,2,0,1:T(8,128)(2,1)} async-done(((bf16[2,8,448,1024]{3,2,0,1:T(8,128)(2,1)}), bf16[2,8,448,1024]{3,2,0,1:T(8,128)(2,1)}, u32[]{:S(2)}, u32[]{:S(2)}) %all-to-all-start) | async-done | bytes 14680096 | tf_op jit(solution)/shard_map/all_to_all | solution.py:42
  406.0 2.7 all-to-all-start.5
  408.7 13.5 %copy.59 = bf16[2,8,448,1024]{3,2,1,0:T(8,128)(2,1)} copy(bf16[2,8,448,1024]{3,2,0,1:T(8,128)(2,1)} %all-to-all-done) | data formatting | bytes 29360128 | tf_op jit(solution)/shard_map/all_to_all | solution.py:42
  422.2 9.3 %gather_fusion = bf16[8,448,1024]{2,1,0:T(8,128)(2,1)} fusion(bf16[16,448,1024]{2,1,0:T(8,128)(2,1)} %bitcast.55, s32[1024]{0:T(1024)S(1)} %pad_clamp_fusion), kind=kCustom, calls=%fused_computation | custom fusion | bytes 14680096 | tf_op jit(solution)/shard_map/gather | solution.py:29
  431.4 5.8 all-to-all-start.1
  437.6 8.3 %mul.65 = f32[28,128,8,128]{3,2,1,0:T(8,128)} broadcast(f32[28,8]{1,0:T(8,128)S(1)} %copy.68), dimensions={0,2} | broadcast | bytes 14680960 | tf_op jit(solution)/shard_map/mul | solution.py:14
  445.9 6.2 mul.68
  452.1 19.5 %fusion.8 = (bf16[3584,1024]{1,0:T(8,128)(2,1)}, bf16[3584,1024]{1,0:T(8,128)(2,1)}) fusion(f32[448,8,8,128]{3,2,1,0:T(8,128)} %bitcast.52, bf16[2,3584,1024]{2,1,0:T(8,128)(2,1)S(1)} %bitcast.51, f32[448,8,8,128]{3,2,1,0:T(8,128)} %bitcast.53), kind=kLoop, calls=%fused_computation.13 | loop fusion | flops 22020096 | bytes 58720256 | tf_op jit(solution)/shard_map/convert_element_type | solution.py:15
  471.6 0.2 compare_reduce_fusion.2
  471.8 0.1 eq.171
  471.9 0.1 eq.168
  472.0 0.1 eq.162
  472.1 0.6 bitcast_convert_fusion
  472.8 0.2 reshape.323
  473.0 125.3 %all-to-all-done.1 = bf16[8,448,1024]{2,1,0:T(8,128)(2,1)} async-done(((bf16[8,448,1024]{2,1,0:T(8,128)(2,1)}), bf16[8,448,1024]{2,1,0:T(8,128)(2,1)}, u32[]{:S(2)}, u32[]{:S(2)}) %all-to-all-start.1) | async-done | bytes 7340064 | tf_op jit(solution)/shard_map/all_to_all | solution.py:47
  598.2 1.0 mul.71
  599.3 8.9 %fusion.6 = bf16[3584,1024]{1,0:T(8,128)(2,1)} fusion(f32[448,8,8,128]{3,2,1,0:T(8,128)S(1)} %bitcast.54, bf16[8,448,1024]{2,1,0:T(8,128)(2,1)} %all-to-all-done.1), kind=kLoop, calls=%fused_computation.9 | loop fusion | flops 11010048 | bytes 29360128 | tf_op jit(solution)/shard_map/convert_element_type | solution.py:15
  608.2 9.3 %fusion = f32[64,3072]{1,0:T(8,128)S(1)} fusion(bf16[64,3584]{1,0:T(8,128)(2,1)S(1)} %reshape.323, bf16[3584,1024]{1,0:T(8,128)(2,1)} %fusion.6, bf16[3584,1024]{1,0:T(8,128)(2,1)} %get-tuple-element.12, bf16[3584,1024]{1,0:T(8,128)(2,1)} %get-tuple-element.11), kind=kOutput, calls=%fused_computation.2 | convolution fusion | flops 1475346432 | bytes 23265280 | tf_op jit(solution)/shard_map/dot_general | solution.py:85
  617.5 0.2 multiply_convert_fusion
  617.7 0.7 reshape.324
  618.4 3.7 all-to-all-start.6
  622.1 0.2 fusion.16
  622.3 40.5 %all-reduce.1 = f32[32,3]{1,0:T(8,128)S(1)} all-reduce(f32[32,3]{1,0:T(8,128)S(1)} %fusion.16), channel_id=2, replica_groups=mesh['group'=4,'dev'=8] {'group','dev'}, use_global_device_ids=true, to_apply=%region_5.6.clone | all-reduce | flops 96 | bytes 768
  662.8 0.5 dynamic-slice_convert_fusion
  663.4 1.0 fusion.10
  664.4 7.0 %copy.81 = bf16[1,3584,1024]{2,1,0:T(8,128)(2,1)} copy(bf16[1,3584,1024]{2,1,0:T(8,128)(2,1)} %bitcast.2) | data formatting | bytes 14680064
  (45 shorter events, 1.1 us)
Async XLA Ops:
  0.6 88.0 %copy-start = (bf16[16,3584]{1,0:T(8,128)(2,1)S(1)}, bf16[16,3584]{1,0:T(8,128)(2,1)}, u32[]{:S(2)}) copy-start(bf16[16,3584]{1,0:T(8,128)(2,1)} %param.10) | copy-start | bytes 344068
  2.8 51.1 %all-to-all-start.2 = ((bf16[8,2,224]{2,1,0:T(2,128)(2,1)}), bf16[8,2,224]{2,1,0:T(2,128)(2,1)S(1)}, u32[]{:S(2)}, u32[]{:S(2)}) async-start(bf16[8,2,224]{2,1,0:T(2,128)(2,1)} %reshape.356), calls=%async_computation.2 | async-start | bytes 16384 | tf_op jit(solution)/shard_map/all_to_all | solution.py:43
  54.0 11.5 %all-to-all-start.4 = ((bf16[32,1,2]{2,1,0:T(2,128)(2,1)}), bf16[32,1,2]{2,1,0:T(2,128)(2,1)S(1)}, u32[]{:S(2)}, u32[]{:S(2)}) async-start(bf16[32,1,2]{2,1,0:T(2,128)(2,1)} %convert_element_type.161), calls=%async_computation.4 | async-start | bytes 32768 | tf_op jit(solution)/shard_map/all_to_all | solution.py:81
  65.4 16.8 %all-to-all-start.3 = ((bf16[8,28,8]{1,2,0:T(8,128)(2,1)}), bf16[8,28,8]{1,2,0:T(8,128)(2,1)S(1)}, u32[]{:S(2)}, u32[]{:S(2)}) async-start(bf16[8,28,8]{1,2,0:T(8,128)(2,1)} %gather_fusion.1), calls=%async_computation.3 | async-start | bytes 32768 | tf_op jit(solution)/shard_map/all_to_all | solution.py:48
  82.2 323.7 %all-to-all-start = ((bf16[2,8,448,1024]{3,2,0,1:T(8,128)(2,1)}), bf16[2,8,448,1024]{3,2,0,1:T(8,128)(2,1)}, u32[]{:S(2)}, u32[]{:S(2)}) async-start(bf16[2,8,448,1024]{3,2,0,1:T(8,128)(2,1)} %copy.58), calls=%async_computation | async-start | bytes 29360128 | tf_op jit(solution)/shard_map/all_to_all | solution.py:42
  406.0 25.5 %all-to-all-start.5 = ((bf16[32,2,3584]{2,1,0:T(2,128)(2,1)}), bf16[32,2,3584]{2,1,0:T(2,128)(2,1)S(1)}, u32[]{:S(2)}, u32[]{:S(2)}) async-start(bf16[32,2,3584]{2,1,0:T(2,128)(2,1)} %reshape.322), calls=%async_computation.5 | async-start | bytes 917504 | tf_op jit(solution)/shard_map/all_to_all | solution.py:78
  422.1 15.1 %copy-start.2 = (bf16[2,28,8]{1,2,0:T(8,128)(2,1)S(1)}, bf16[2,28,8]{1,2,0:T(8,128)(2,1)}, u32[]{:S(2)}) copy-start(bf16[2,28,8]{1,2,0:T(8,128)(2,1)} %param.8) | copy-start | bytes 2692
  422.1 15.3 %copy-start.3 = (s32[16,8]{0,1:T(8,128)S(1)}, s32[16,8]{0,1:T(8,128)}, u32[]{:S(2)}) copy-start(s32[16,8]{0,1:T(8,128)} %param.13) | copy-start | bytes 1540
  431.4 166.8 %all-to-all-start.1 = ((bf16[8,448,1024]{2,1,0:T(8,128)(2,1)}), bf16[8,448,1024]{2,1,0:T(8,128)(2,1)}, u32[]{:S(2)}, u32[]{:S(2)}) async-start(bf16[8,448,1024]{2,1,0:T(8,128)(2,1)} %gather_fusion), calls=%async_computation.1 | async-start | bytes 14680064 | tf_op jit(solution)/shard_map/all_to_all | solution.py:47
  437.6 14.5 %slice-start = ((s8[14680064]{0:T(1024)(128)(4,1)}), s8[2097152]{0:T(1024)(128)(4,1)S(1)}, s32[]{:S(2)}) async-start(s8[14680064]{0:T(1024)(128)(4,1)} %bitcast.50), calls=%async_computation.7 | async-start | bytes 4194304
  437.6 14.5 %slice-start.1 = ((s8[14680064]{0:T(1024)(128)(4,1)}), s8[4194304]{0:T(1024)(128)(4,1)S(1)}, s32[]{:S(2)}) async-start(s8[14680064]{0:T(1024)(128)(4,1)} %bitcast.50), calls=%async_computation.8 | async-start | bytes 8388608
  437.6 14.5 %slice-start.2 = ((s8[14680064]{0:T(1024)(128)(4,1)}), s8[4194304]{0:T(1024)(128)(4,1)S(1)}, s32[]{:S(2)}) async-start(s8[14680064]{0:T(1024)(128)(4,1)} %bitcast.50), calls=%async_computation.9 | async-start | bytes 8388608
  445.9 6.2 slice-start.3
  608.2 63.1 %copy-start.1 = (bf16[16,3584]{1,0:T(8,128)(2,1)S(1)}, bf16[16,3584]{1,0:T(8,128)(2,1)}, u32[]{:S(2)}) copy-start(bf16[16,3584]{1,0:T(8,128)(2,1)} %param.10) | copy-start | bytes 344068
  618.4 44.9 %all-to-all-start.6 = ((bf16[32,2,1024]{2,1,0:T(2,128)(2,1)}), bf16[32,2,1024]{2,1,0:T(2,128)(2,1)S(1)}, u32[]{:S(2)}, u32[]{:S(2)}) async-start(bf16[32,2,1024]{2,1,0:T(2,128)(2,1)} %reshape.324), calls=%async_computation.6 | async-start | bytes 262144 | tf_op jit(solution)/shard_map/all_to_all | solution.py:104
where the time goes:
time: 672 us; the launch traced here: 671 us
  waiting for transfers between devices  447 us (67%)
  blocking collectives  81.3 us (12%)
  local copies, waits for them, and re-layouts  66.8 us (10%)
  starting transfers between devices  33.1 us (5%)
  other arithmetic  30.6 us (5%)
  matrix products  10.8 us (2%)
    all_to_all x1, waiting for transfers between devices, per_device(): lax.all_to_all(split_values, 'dev', split_axis=1, concat_axis=1, tiled=True)  316 us
    all_to_all x1, waiting for transfers between devices, per_device(): lax.all_to_all(send_values, 'dev', split_axis=0, concat_axis=0, tiled=True)  125 us
    unnamed x2, blocking collectives  81.3 us
    convert_element_type x2, other arithmetic, dequantize(): return scaled.reshape(D, FF).astype(jnp.bfloat16)  28.4 us
    mul x3, local copies, waits for them, and re-layouts, dequantize(): scaled = tile_grid * scales.astype(jnp.float32)[:, None, :, None]  15.5 us
    reshape x1, local copies, waits for them, and re-layouts, spread_parts(): values.reshape(holding, parts_count, width_in // parts_count, hidden)  13.5 us
    all_to_all x1, local copies, waits for them, and re-layouts, per_device(): lax.all_to_all(split_values, 'dev', split_axis=1, concat_axis=1, tiled=True)  13.5 us
  transfers between devices with their start and end apart: 7, of which 3 were waited for; matrix products, arithmetic and copies ran while one was open for 12% of the time, Pallas kernels for 0%

commit v1 on v0

v1 whole, which is shorter than its diff:
```python
import functools

import jax
import jax.numpy as jnp
from jax import lax
from jax.experimental import pallas as pl
from jax.experimental.pallas import tpu as pltpu
from jax.sharding import PartitionSpec as P

TILE = 128
CAP = 2
POOL = 16
AXES = ("group", "dev")
PARTS = (128, 96)


def expert_kernel(x_ref, q_ref, s_ref, o_ref, acc_ref):
    step = pl.program_id(0)

    @pl.when(step == 0)
    def _():
        acc_ref[...] = jnp.zeros_like(acc_ref)

    holding, depth, _ = q_ref.shape
    cells = 2 * CAP
    rows = x_ref.shape[0]
    member_of = lax.broadcasted_iota(jnp.int32, (rows, TILE), 0) // cells % holding
    total = acc_ref[...]
    for member in range(holding):
        for block in range(depth // TILE):
            span = slice(block * TILE, (block + 1) * TILE)
            scale = s_ref[member, 0, block : block + 1, :]
            weights = (q_ref[member, span, :].astype(jnp.float32) * scale).astype(jnp.bfloat16)
            rows_in = jnp.where(member_of == member, x_ref[:, span], jnp.zeros((), jnp.bfloat16))
            total = total + jnp.dot(rows_in, weights, preferred_element_type=jnp.float32)
    acc_ref[...] = total

    @pl.when(step == pl.num_programs(0) - 1)
    def _():
        value = acc_ref[...]
        o_ref[...] = (value / (1.0 + jnp.exp(-value))).astype(jnp.bfloat16)


def serve(rows, values, scales):
    holding, width_in, hidden = values.shape
    depth = 512
    steps = width_in // depth
    count = rows.shape[0]
    wide = jnp.repeat(scales.astype(jnp.float32), TILE, axis=2)
    wide = wide.reshape(holding, steps, depth // TILE, hidden)
    return pl.pallas_call(
        expert_kernel,
        grid=(steps,),
        in_specs=[
            pl.BlockSpec((count, depth), lambda k: (0, k)),
            pl.BlockSpec((holding, depth, hidden), lambda k: (0, k, 0)),
            pl.BlockSpec((holding, 1, depth // TILE, hidden), lambda k: (0, k, 0, 0)),
        ],
        out_specs=pl.BlockSpec((count, hidden), lambda k: (0, 0)),
        out_shape=jax.ShapeDtypeStruct((count, hidden), jnp.bfloat16),
        scratch_shapes=[pltpu.VMEM((count, hidden), jnp.float32)],
        compiler_params=pltpu.CompilerParams(vmem_limit_bytes=48 * 1024 * 1024),
        cost_estimate=pl.CostEstimate(
            flops=2 * count * width_in * hidden * holding,
            bytes_accessed=2 * (values.size + rows.size + count * hidden),
            transcendentals=count * hidden,
        ),
    )(rows, values, wide)


def gather_kernel(count, index_ref, near_ref, far_ref, out_ref, sem):
    near_count = near_ref.shape[0]

    def step(spot, carry):
        index = index_ref[spot]

        @pl.when(index < near_count)
        def _():
            pltpu.make_async_copy(
                near_ref.at[jnp.minimum(index, near_count - 1)], out_ref.at[spot], sem
            ).start()

        @pl.when(index >= near_count)
        def _():
            far_index = jnp.maximum(index - near_count, 0)
            pltpu.make_async_copy(far_ref.at[far_index], out_ref.at[spot], sem).start()

        return carry

    lax.fori_loop(0, count, step, 0)
    pltpu.make_async_copy(out_ref, out_ref, sem).wait()


def gather(indices, near, far):
    count = indices.shape[0]
    anywhere = pl.BlockSpec(memory_space=pl.ANY)
    return pl.pallas_call(
        functools.partial(gather_kernel, count),
        in_specs=[pl.BlockSpec(memory_space=pltpu.SMEM), anywhere, anywhere],
        out_specs=anywhere,
        out_shape=jax.ShapeDtypeStruct((count,) + near.shape[1:], near.dtype),
        scratch_shapes=[pltpu.SemaphoreType.DMA],
    )(indices, near, far)


def cross_over(count, blocks, pairs):
    most = blocks.shape[0]

    def branch_of(size):
        def branch(held):
            if size == 0:
                return jnp.zeros_like(held)
            got = lax.ppermute(held[:size], AXES, pairs)
            return jnp.pad(got, ((0, most - size), (0, 0), (0, 0)))

        return branch

    return lax.switch(count, [branch_of(size) for size in range(most + 1)], blocks)


def per_device(primary_q, primary_scales, new_place, tokens, experts, replica, route_num):
    holding, width_in, hidden = primary_q.shape
    dev_count = lax.axis_size("dev")
    group_count = lax.axis_size("group")
    device_count = dev_count * group_count
    half = dev_count // 2
    pooled = POOL // half
    my_dev = lax.axis_index("dev")
    my_group = lax.axis_index("group")
    first_dev = my_group * dev_count
    pools = [
        [(base + group) * dev_count + side * half + spot for group in range(pooled) for spot in range(half)]
        for base in range(0, group_count, pooled)
        for side in range(2)
    ]
    over = [
        (group * dev_count + spot, group * dev_count + (spot + half) % dev_count)
        for group in range(group_count)
        for spot in range(dev_count)
    ]

    scale_count = primary_scales.size
    notice = jnp.concatenate(
        [primary_scales.reshape(scale_count), new_place.astype(jnp.bfloat16)]
    )
    notice = jnp.pad(notice, (0, -notice.size % TILE))
    notices = lax.all_to_all(
        jnp.broadcast_to(notice[None], (device_count, notice.size)),
        AXES,
        split_axis=0,
        concat_axis=0,
        tiled=True,
    )

    spread = []
    start = 0
    for height in PARTS:
        block = primary_q[:, start : start + POOL * height]
        block = block.reshape(holding, POOL, height, hidden).transpose(1, 0, 2, 3)
        block = lax.all_to_all(
            block, AXES, split_axis=0, concat_axis=0, tiled=True, axis_index_groups=pools
        )
        spread.append(block.reshape(POOL * holding, height, hidden))
        start += POOL * height

    place_all = notices[:, scale_count].astype(jnp.int32)
    nearby = lax.dynamic_slice_in_dim(notices, first_dev, dev_count)
    wanted = lax.dynamic_slice_in_dim(place_all, first_dev, dev_count)
    owner = wanted // holding - first_dev
    member = wanted % holding
    own_scales = lax.dynamic_slice(
        nearby[:, :scale_count].reshape(dev_count * holding, scale_count // holding),
        (owner[my_dev] * holding + member[my_dev], 0),
        (1, scale_count // holding),
    )
    new_scales = own_scales.reshape((1,) + primary_scales.shape[1:])

    row_count, top_count = experts.shape
    pair_count = row_count * top_count
    expert_flat = experts.reshape(pair_count)
    device_ids = jnp.arange(device_count, dtype=jnp.int32)
    matched = expert_flat[:, None] == place_all[None, :]
    has_copy = jnp.any(matched, axis=1)
    holder = jnp.sum(jnp.where(matched, device_ids[None, :], 0), axis=1)
    use_copy = (replica.reshape(pair_count) == 1) & has_copy
    target = jnp.where(use_copy, holder, expert_flat // holding)
    slot_id = jnp.where(use_copy, holding, expert_flat % holding)
    pair_order = jnp.arange(pair_count)
    before = pair_order[None, :] < pair_order[:, None]
    position = jnp.sum((target[:, None] == target[None, :]) & before, axis=1)
    served = position < CAP
    cells = 2 * CAP
    same_expert = (expert_flat[:, None] == expert_flat[None, :]) & before & served[None, :]
    cell_index = expert_flat * cells + jnp.sum(same_expert, axis=1)
    cell_count = device_count * holding * cells
    placed = (cell_index[None, :] == jnp.arange(cell_count)[:, None]) & served[None, :]
    row_hits = jnp.any(placed.reshape(cell_count, row_count, top_count), axis=2)
    row_buffer = jnp.dot(row_hits.astype(jnp.bfloat16), tokens, preferred_element_type=jnp.float32)
    row_buffer = row_buffer.astype(jnp.bfloat16).reshape(device_count, holding * cells, width_in)
    row_block = lax.all_to_all(row_buffer, AXES, split_axis=0, concat_axis=0, tiled=True)

    dest_hit = (target[None, :] == device_ids[:, None]) & served[None, :]
    slot_hit = slot_id[:, None] == jnp.arange(holding + 1)[None, :]
    counted = jnp.dot(
        dest_hit.astype(jnp.bfloat16),
        slot_hit.astype(jnp.bfloat16),
        preferred_element_type=jnp.float32,
    )
    counts = lax.all_to_all(
        counted.astype(jnp.bfloat16), AXES, split_axis=0, concat_axis=0, tiled=True
    )
    slot_load = jnp.sum(counts.astype(jnp.float32), axis=0, keepdims=True).astype(jnp.int32)

    activated = serve(row_block.reshape(cell_count, width_in), primary_q, primary_scales)
    returned = lax.all_to_all(
        activated.reshape(device_count, holding * cells, hidden),
        AXES,
        split_axis=0,
        concat_axis=0,
        tiled=True,
    )
    selected = jnp.dot(
        placed.T.astype(jnp.bfloat16),
        returned.reshape(cell_count, hidden),
        preferred_element_type=jnp.float32,
    )
    weight = route_num.reshape(pair_count).astype(jnp.float32) / 16.0
    hidden_out = (selected * weight[:, None]).astype(jnp.bfloat16)
    hidden_out = hidden_out.reshape(row_count, top_count, hidden)

    source = place_all // holding
    dest_side = device_ids % dev_count // half
    source_side = source % dev_count // half
    crossing = source_side != dest_side
    row_at = (source // dev_count % pooled * half + source % half) * holding + place_all % holding
    pool_of = device_ids // dev_count // pooled
    peers = (pool_of[:, None] == pool_of[None, :]) & (dest_side[:, None] == dest_side[None, :])
    ahead = peers & crossing[None, :] & (device_ids[None, :] < device_ids[:, None])
    rank = jnp.sum(ahead, axis=1)
    cross_count = jnp.max(jnp.where(crossing, rank + 1, 0))
    my_side = my_dev // half
    my_pool = my_group // pooled
    leaving = (pool_of == my_pool) & (dest_side != my_side) & crossing
    slots = jnp.arange(POOL)
    leave_rows = jnp.sum(
        jnp.where(leaving[None, :] & (rank[None, :] == slots[:, None]), row_at[None, :], 0), axis=1
    )
    staying = (pool_of == my_pool) & (dest_side == my_side)
    place_in_pool = device_ids // dev_count % pooled * half + device_ids % half
    give_rows = jnp.sum(
        jnp.where(
            staying[None, :] & (place_in_pool[None, :] == slots[:, None]),
            jnp.where(crossing, POOL * holding + rank, row_at)[None, :],
            0,
        ),
        axis=1,
    )
    pieces = []
    for block in spread:
        arrived = cross_over(cross_count, gather(leave_rows, block, block), over)
        given = gather(give_rows, block, arrived)
        given = lax.all_to_all(
            given, AXES, split_axis=0, concat_axis=0, tiled=True, axis_index_groups=pools
        )
        pieces.append(given.reshape(1, -1, hidden))
    new_weights = jnp.concatenate(pieces, axis=1)
    return (new_weights, new_scales, hidden_out, slot_load)


def solution(mesh):
    in_specs = (
        P(AXES, None, None),
        P(AXES, None, None),
        P(AXES),
        P(AXES, None),
        P(AXES, None),
        P(AXES, None),
        P(AXES, None),
    )
    out_specs = (
        P(AXES, None, None),
        P(AXES, None, None),
        P(AXES, None, None),
        P(AXES, None),
    )
    return jax.shard_map(
        per_device, mesh=mesh, in_specs=in_specs, out_specs=out_specs, check_vma=False
    )
```

time: 672 us -> 884 us (1.32)
  Pallas kernels: 0 us -> 371 us
  blocking collectives: 81.3 us -> 0 us
  local copies, waits for them, and re-layouts: 66.8 us -> 36.3 us
  waiting for transfers between devices: 447 us -> 417 us
  other arithmetic: 30.6 us -> 11.4 us
    pallas_call x0 -> x5, Pallas kernels: none -> 371 us  [the longest x4 358 us: gather(): pl.pallas_call(functools.partial(gather_kernel, count), in_specs=[pl.Bloc...]
    all_to_all x7 -> x8, waiting for transfers between devices: 447 us -> 167 us  [the longest x2 62.1 us: per_device(): lax.all_to_all(block, AXES, split_axis=0, concat_axis=0, tiled=True, axis...]
    ppermute x0 -> x2, waiting for transfers between devices: none -> 250 us  [branch(): got = lax.ppermute(held[:size], AXES, pairs)]
    unnamed x2 -> x0, blocking collectives: 81.3 us -> none
    convert_element_type x7 -> x3, other arithmetic: 29.7 us -> 0.78 us  [the longest x1 0.52 us: per_device(): jnp.sum(counts.astype(jnp.float32), axis=0, keepdims=True).astype(jnp.int32)]
    mul x3 -> x0, local copies, waits for them, and re-layouts: 15.5 us -> none  [dequantize(): scaled = tile_grid * scales.astype(jnp.float32)[:, None, :, None]]
    all_to_all x2 -> x1, local copies, waits for them, and re-layouts: 13.5 us -> 0.73 us  [per_device(): lax.all_to_all(counted.astype(jnp.bfloat16), AXES, split_axis=0, concat_a...]
    slice x0 -> x5, local copies, waits for them, and re-layouts: none -> 12.5 us  [the longest x3 10.4 us: per_device(): block = primary_q[:, start:start + POOL * height]]
  transfers between devices with their start and end apart: 7 -> 10, of which waited for: 3 -> 7; matrix products, arithmetic and copies ran while one was open for 12% -> 4% of each run, Pallas kernels for 0% -> 42%
where the time goes in v1:
time: 884 us; the launch traced here: 883 us
  waiting for transfers between devices  417 us (47%)
  Pallas kernels  371 us (42%)
  starting transfers between devices  39.9 us (5%)
  local copies, waits for them, and re-layouts  36.3 us (4%)
  other arithmetic  11.4 us (1%)
    pallas_call x4, Pallas kernels, gather(): pl.pallas_call(functools.partial(gather_kernel, count), in_specs=[pl.Bloc...  358 us
    ppermute x2, waiting for transfers between devices, branch(): got = lax.ppermute(held[:size], AXES, pairs)  250 us
    all_to_all x2, waiting for transfers between devices, per_device(): lax.all_to_all(block, AXES, split_axis=0, concat_axis=0, tiled=True, axis...  62.1 us
    all_to_all x2, waiting for transfers between devices, per_device(): lax.all_to_all(given, AXES, split_axis=0, concat_axis=0, tiled=True, axis...  46.2 us
    all_to_all x1, waiting for transfers between devices, per_device(): lax.all_to_all(row_buffer, AXES, split_axis=0, concat_axis=0, tiled=True)  43.1 us
  transfers between devices with their start and end apart: 10, of which 7 were waited for; matrix products, arithmetic and copies ran while one was open for 4% of the time, Pallas kernels for 42%

profile of v1, /device:TPU:0, one launch (start us, length us, event | category | flops | bytes accessed | tf_op | source)
XLA Modules:
  0.0 883.1 jit_solution(18005838286624143085)
XLA Ops:
  0.7 0.8 copy.67
  2.4 0.5 broadcast.1154
  2.9 0.8 reduce.7
  3.7 0.6 reshape.501
  4.4 7.3 all-to-all-start
  11.7 0.7 broadcast_compare_fusion
  12.4 0.8 copy.71
  13.4 5.5 all-to-all-done
  20.0 1.9 fusion
  21.9 2.7 all-to-all-start.5
  25.2 0.7 copy.76
  25.9 43.1 %all-to-all-done.5 = bf16[32,8,3584]{2,1,0:T(8,128)(2,1)S(1)} async-done(((bf16[32,8,3584]{2,1,0:T(8,128)(2,1)}), bf16[32,8,3584]{2,1,0:T(8,128)(2,1)S(1)}, u32[]{:S(2)}, u32[]{:S(2)}) %all-to-all-start.5) | async-done | bytes 1835040 | tf_op jit(solution)/shard_map/all_to_all | solution.py:200
  69.1 2.9 all-to-all-start.7
  71.9 12.7 %shard_map.106 = bf16[256,1024]{1,0:T(8,128)(2,1)} custom-call(bf16[256,3584]{1,0:T(8,128)(2,1)S(1)} %bitcast.37, bf16[2,3584,1024]{2,1,0:T(8,128)(2,1)} %q_ref.1, f32[2,7,4,1024]{3,2,1,0:T(4,128)S(1)} %reshape_reshape.3.s_ref), custom_call_target="tpu_custom_call" | custom-call | flops 3758096384 | bytes 17039360 | tf_op jit(solution)/shard_map/pallas_call | solution.py:51
  84.6 5.8 all-to-all-start.6
  90.5 2.8 slice-done
  93.2 3.4 copy.85
  96.7 10.1 %all-to-all-done.6 = bf16[32,8,1024]{2,1,0:T(8,128)(2,1)S(1)} async-done(((bf16[32,8,1024]{2,1,0:T(8,128)(2,1)}), bf16[32,8,1024]{2,1,0:T(8,128)(2,1)S(1)}, u32[]{:S(2)}, u32[]{:S(2)}) %all-to-all-start.6) | async-done | bytes 524320 | tf_op jit(solution)/shard_map/all_to_all | solution.py:215
  106.8 0.8 copy-done.2
  107.6 4.7 all-to-all-start.3
  112.3 7.6 slice.103
  119.9 8.2 copy.84
  128.1 62.1 %all-to-all-done.3 = bf16[16,2,96,1024]{3,2,1,0:T(8,128)(2,1)} async-done(((bf16[16,2,96,1024]{3,2,1,0:T(8,128)(2,1)}), bf16[16,2,96,1024]{3,2,1,0:T(8,128)(2,1)}, u32[]{:S(2)}, u32[]{:S(2)}) %all-to-all-start.3) | async-done | bytes 6291488 | tf_op jit(solution)/shard_map/all_to_all | solution.py:160
  190.2 4.7 all-to-all-start.1
  195.3 0.6 add_select_fusion
  196.6 0.6 select_reduce_fusion.index_ref
  197.2 0.6 select_reduce_fusion.1.index_ref
  197.8 3.2 shard_map.104
  201.1 138.6 %conditional.3 = (bf16[16,96,1024]{2,1,0:T(8,128)(2,1)}) conditional(s32[]{:T(128)} %clamp.4, () %tuple.111, bf16[16,96,1024]{2,1,0:T(8,128)(2,1)S(1)} %shard_map.104, bf16[16,96,1024]{2,1,0:T(8,128)(2,1)S(1)} %shard_map.104, bf16[16,96,1024]{2,1,0:T(8,128)(2,1)S(1)} %shard_map.104, ...), branch_computations={%region_21.22_spmd, %region_22.23_spmd, %region_23.24_spmd, %regio... | conditional | bytes 23789618 | solution.py:118
  201.4 136.2 %collective-permute-done.25 = bf16[10,96,1024]{2,1,0:T(8,128)(2,1)S(1)} collective-permute-done((bf16[10,96,1024]{2,1,0:T(8,128)(2,1)S(1)}, bf16[10,96,1024]{2,1,0:T(8,128)(2,1)S(1)}, u32[]{:S(2)}, u32[]{:S(2)}) %collective-permute-start.25) | collective-permute-done | bytes 1966112 | tf_op jit(solution)/shard_map/cond/branch_10_fun/ppermute | solution.py:113
  337.6 2.1 pad.117
  339.7 97.1 %shard_map.105 = bf16[16,96,1024]{2,1,0:T(8,128)(2,1)} custom-call(s32[16]{0:T(128)} %select_reduce_fusion.1.index_ref, bf16[32,96,1024]{2,1,0:T(8,128)(2,1)} %bitcast.6.near_ref.far_ref, bf16[16,96,1024]{2,1,0:T(8,128)(2,1)} %get-tuple-element.109.far_ref), custom_call_target="tpu_custom_call" | custom-call | tf_op jit(solution)/shard_map/pallas_call | solution.py:97
  436.8 3.8 all-to-all-start.4
  440.6 128.8 %shard_map.102 = bf16[16,128,1024]{2,1,0:T(8,128)(2,1)} custom-call(s32[16]{0:T(128)} %select_reduce_fusion.index_ref, bf16[32,128,1024]{2,1,0:T(8,128)(2,1)} %bitcast.2.near_ref.far_ref, bf16[32,128,1024]{2,1,0:T(8,128)(2,1)} %bitcast.2.near_ref.far_ref), custom_call_target="tpu_custom_call" | custom-call | tf_op jit(solution)/shard_map/pallas_call | solution.py:97
  569.4 121.5 %conditional.2 = (bf16[16,128,1024]{2,1,0:T(8,128)(2,1)}) conditional(s32[]{:T(128)} %clamp.4, () %tuple.110, bf16[16,128,1024]{2,1,0:T(8,128)(2,1)} %shard_map.102, bf16[16,128,1024]{2,1,0:T(8,128)(2,1)} %shard_map.102, bf16[16,128,1024]{2,1,0:T(8,128)(2,1)} %shard_map.102, ...), branch_computations={%region_4.5_spmd, %region_5.6_spmd, %region_6.7_spmd, %region_7.8_... | conditional | bytes 31719474 | solution.py:118
  569.4 2.0 slice.77
  571.5 3.4 collective-permute-start.9
  574.9 113.5 %collective-permute-done.9 = bf16[10,128,1024]{2,1,0:T(8,128)(2,1)S(1)} collective-permute-done((bf16[10,128,1024]{2,1,0:T(8,128)(2,1)S(1)}, bf16[10,128,1024]{2,1,0:T(8,128)(2,1)S(1)}, u32[]{:S(2)}, u32[]{:S(2)}) %collective-permute-start.9) | collective-permute-done | bytes 2621472 | tf_op jit(solution)/shard_map/cond/branch_10_fun/ppermute | solution.py:113
  688.4 2.5 pad.102
  690.9 128.8 %shard_map.103 = bf16[16,128,1024]{2,1,0:T(8,128)(2,1)} custom-call(s32[16]{0:T(128)} %select_reduce_fusion.1.index_ref, bf16[32,128,1024]{2,1,0:T(8,128)(2,1)} %bitcast.2.near_ref.far_ref, bf16[16,128,1024]{2,1,0:T(8,128)(2,1)} %get-tuple-element.108.far_ref), custom_call_target="tpu_custom_call" | custom-call | tf_op jit(solution)/shard_map/pallas_call | solution.py:97
  819.8 4.6 all-to-all-start.2
  824.7 0.6 dynamic_slice.23
  825.3 0.6 dynamic_slice.24
  827.5 0.7 copy.77
  828.2 0.5 convert_bitcast_fusion
  828.7 2.0 fusion.2
  830.7 46.2 %all-to-all-done.2 = bf16[16,128,1024]{2,1,0:T(8,128)(2,1)} async-done(((bf16[16,128,1024]{2,1,0:T(8,128)(2,1)}), bf16[16,128,1024]{2,1,0:T(8,128)(2,1)}, u32[]{:S(2)}, u32[]{:S(2)}) %all-to-all-start.2) | async-done | bytes 4194336 | tf_op jit(solution)/shard_map/all_to_all | solution.py:262
  876.9 6.1 pad_maximum_fusion
  (56 shorter events, 3.3 us)
Async XLA Ops:
  0.6 19.4 %copy-start = (bf16[16,3584]{1,0:T(8,128)(2,1)S(1)}, bf16[16,3584]{1,0:T(8,128)(2,1)}, u32[]{:S(2)}) copy-start(bf16[16,3584]{1,0:T(8,128)(2,1)} %param.44) | copy-start | bytes 344068
  0.6 24.0 %copy-start.3 = (bf16[2,28,8]{1,2,0:T(8,128)(2,1)S(1)}, bf16[2,28,8]{1,2,0:T(8,128)(2,1)}, u32[]{:S(2)}) copy-start(bf16[2,28,8]{1,2,0:T(8,128)(2,1)} %param.42) | copy-start | bytes 2692
  4.4 14.5 %all-to-all-start = ((bf16[32,2,256]{2,1,0:T(2,128)(2,1)}), bf16[32,2,256]{2,1,0:T(2,128)(2,1)S(1)}, u32[]{:S(2)}, u32[]{:S(2)}) async-start(bf16[32,2,256]{2,1,0:T(2,128)(2,1)} %reshape.501), calls=%async_computation | async-start | bytes 65536 | tf_op jit(solution)/shard_map/all_to_all | solution.py:147
  21.9 47.2 %all-to-all-start.5 = ((bf16[32,8,3584]{2,1,0:T(8,128)(2,1)}), bf16[32,8,3584]{2,1,0:T(8,128)(2,1)S(1)}, u32[]{:S(2)}, u32[]{:S(2)}) async-start(bf16[32,8,3584]{2,1,0:T(8,128)(2,1)} %fusion), calls=%async_computation.5 | async-start | bytes 3670016 | tf_op jit(solution)/shard_map/all_to_all | solution.py:200
  69.1 15.5 %all-to-all-start.7 = ((bf16[32,1,3]{2,1,0:T(2,128)(2,1)}), bf16[32,1,3]{2,1,0:T(2,128)(2,1)S(1)}, u32[]{:S(2)}, u32[]{:S(2)}) async-start(bf16[32,1,3]{2,1,0:T(2,128)(2,1)} %copy.76), calls=%async_computation.7 | async-start | bytes 32768 | tf_op jit(solution)/shard_map/all_to_all | solution.py:209
  84.6 22.2 %all-to-all-start.6 = ((bf16[32,8,1024]{2,1,0:T(8,128)(2,1)}), bf16[32,8,1024]{2,1,0:T(8,128)(2,1)S(1)}, u32[]{:S(2)}, u32[]{:S(2)}) async-start(bf16[32,8,1024]{2,1,0:T(8,128)(2,1)} %bitcast.12), calls=%async_computation.6 | async-start | bytes 1048576 | tf_op jit(solution)/shard_map/all_to_all | solution.py:215
  90.5 2.8 slice-start
  106.8 0.8 copy-start.2
  107.6 82.6 %all-to-all-start.3 = ((bf16[16,2,96,1024]{3,2,1,0:T(8,128)(2,1)}), bf16[16,2,96,1024]{3,2,1,0:T(8,128)(2,1)}, u32[]{:S(2)}, u32[]{:S(2)}) async-start(bf16[16,2,96,1024]{3,2,1,0:T(8,128)(2,1)} %bitcast.41), calls=%async_computation.3 | async-start | bytes 12582912 | tf_op jit(solution)/shard_map/all_to_all | solution.py:160
  190.2 246.5 %all-to-all-start.1 = ((bf16[16,2,128,1024]{3,2,1,0:T(8,128)(2,1)}), bf16[16,2,128,1024]{3,2,1,0:T(8,128)(2,1)}, u32[]{:S(2)}, u32[]{:S(2)}) async-start(bf16[16,2,128,1024]{3,2,1,0:T(8,128)(2,1)} %bitcast.39), calls=%async_computation.1 | async-start | bytes 16777216 | tf_op jit(solution)/shard_map/all_to_all | solution.py:160
  201.3 136.3 %collective-permute-start.25 = (bf16[10,96,1024]{2,1,0:T(8,128)(2,1)S(1)}, bf16[10,96,1024]{2,1,0:T(8,128)(2,1)S(1)}, u32[]{:S(2)}, u32[]{:S(2)}) collective-permute-start(bf16[10,96,1024]{2,1,0:T(8,128)(2,1)S(1)} %slice.92), channel_id=1, source_target_pairs={{0,4},{1,5},{2,6},{3,7},{4,0},{5,1},{6,2},{7,3},{8,12},{9,13},{10,... | collective-permute-start | bytes 5898248 | tf_op jit(solution)/shard_map/cond/branch_10_fun/ppermute | solution.py:113
  436.8 383.0 %all-to-all-start.4 = ((bf16[16,96,1024]{2,1,0:T(8,128)(2,1)}), bf16[16,96,1024]{2,1,0:T(8,128)(2,1)S(1)}, u32[]{:S(2)}, u32[]{:S(2)}) async-start(bf16[16,96,1024]{2,1,0:T(8,128)(2,1)} %shard_map.105), calls=%async_computation.4 | async-start | bytes 6291456 | tf_op jit(solution)/shard_map/all_to_all | solution.py:262
  571.5 117.0 %collective-permute-start.9 = (bf16[10,128,1024]{2,1,0:T(8,128)(2,1)S(1)}, bf16[10,128,1024]{2,1,0:T(8,128)(2,1)S(1)}, u32[]{:S(2)}, u32[]{:S(2)}) collective-permute-start(bf16[10,128,1024]{2,1,0:T(8,128)(2,1)S(1)} %slice.77), channel_id=1, source_target_pairs={{0,4},{1,5},{2,6},{3,7},{4,0},{5,1},{6,2},{7,3},{8,12},{9,13},{10,... | collective-permute-start | bytes 7864328 | tf_op jit(solution)/shard_map/cond/branch_10_fun/ppermute | solution.py:113
  819.7 4.6 copy-start.4
  819.8 57.2 %all-to-all-start.2 = ((bf16[16,128,1024]{2,1,0:T(8,128)(2,1)}), bf16[16,128,1024]{2,1,0:T(8,128)(2,1)}, u32[]{:S(2)}, u32[]{:S(2)}) async-start(bf16[16,128,1024]{2,1,0:T(8,128)(2,1)} %shard_map.103), calls=%async_computation.2 | async-start | bytes 8388608 | tf_op jit(solution)/shard_map/all_to_all | solution.py:262
  876.9 6.1 copy-start.1

commit v2 on v1

--- a/solution.py
+++ b/solution.py
@@ -11,7 +11,7 @@
 CAP = 2
 POOL = 16
 AXES = ("group", "dev")
-PARTS = (128, 96)
+PARTS = (112, 112)
 
 
 def expert_kernel(x_ref, q_ref, s_ref, o_ref, acc_ref):
@@ -62,7 +62,7 @@
         compiler_params=pltpu.CompilerParams(vmem_limit_bytes=48 * 1024 * 1024),
         cost_estimate=pl.CostEstimate(
             flops=2 * count * width_in * hidden * holding,
-            bytes_accessed=2 * (values.size + rows.size + count * hidden),
+            bytes_accessed=2 * (values.size + count * (width_in + hidden)),
             transcendentals=count * hidden,
         ),
     )(rows, values, wide)
@@ -97,10 +97,25 @@
     return pl.pallas_call(
         functools.partial(gather_kernel, count),
         in_specs=[pl.BlockSpec(memory_space=pltpu.SMEM), anywhere, anywhere],
-        out_specs=anywhere,
+        out_specs=pl.BlockSpec(memory_space=pltpu.VMEM),
         out_shape=jax.ShapeDtypeStruct((count,) + near.shape[1:], near.dtype),
         scratch_shapes=[pltpu.SemaphoreType.DMA],
     )(indices, near, far)
+
+
+def copy_kernel(in_ref, out_ref):
+    out_ref[0] = in_ref[...]
+
+
+def by_chunk(values, first, height):
+    holding, _, hidden = values.shape
+    return pl.pallas_call(
+        copy_kernel,
+        grid=(POOL,),
+        in_specs=[pl.BlockSpec((holding, height, hidden), lambda k: (0, first // height + k, 0))],
+        out_specs=pl.BlockSpec((1, holding, height, hidden), lambda k: (k, 0, 0, 0)),
+        out_shape=jax.ShapeDtypeStruct((POOL, holding, height, hidden), values.dtype),
+    )(values)
 
 
 def cross_over(count, blocks, pairs):
@@ -139,79 +154,80 @@
         for spot in range(dev_count)
     ]
 
-    scale_count = primary_scales.size
-    notice = jnp.concatenate(
-        [primary_scales.reshape(scale_count), new_place.astype(jnp.bfloat16)]
-    )
-    notice = jnp.pad(notice, (0, -notice.size % TILE))
-    notices = lax.all_to_all(
-        jnp.broadcast_to(notice[None], (device_count, notice.size)),
-        AXES,
-        split_axis=0,
-        concat_axis=0,
-        tiled=True,
-    )
-
     spread = []
     start = 0
     for height in PARTS:
-        block = primary_q[:, start : start + POOL * height]
-        block = block.reshape(holding, POOL, height, hidden).transpose(1, 0, 2, 3)
         block = lax.all_to_all(
-            block, AXES, split_axis=0, concat_axis=0, tiled=True, axis_index_groups=pools
+            by_chunk(primary_q, start, height), AXES, split_axis=0, concat_axis=0, tiled=True, axis_index_groups=pools
         )
         spread.append(block.reshape(POOL * holding, height, hidden))
         start += POOL * height
 
-    place_all = notices[:, scale_count].astype(jnp.int32)
-    nearby = lax.dynamic_slice_in_dim(notices, first_dev, dev_count)
-    wanted = lax.dynamic_slice_in_dim(place_all, first_dev, dev_count)
-    owner = wanted // holding - first_dev
-    member = wanted % holding
-    own_scales = lax.dynamic_slice(
-        nearby[:, :scale_count].reshape(dev_count * holding, scale_count // holding),
-        (owner[my_dev] * holding + member[my_dev], 0),
-        (1, scale_count // holding),
-    )
-    new_scales = own_scales.reshape((1,) + primary_scales.shape[1:])
-
     row_count, top_count = experts.shape
     pair_count = row_count * top_count
-    expert_flat = experts.reshape(pair_count)
+    scale_cols = primary_scales.size // row_count
+    notice = jnp.concatenate(
+        [
+            experts.astype(jnp.bfloat16),
+            replica.astype(jnp.bfloat16),
+            jnp.broadcast_to(new_place.astype(jnp.bfloat16)[None], (row_count, 1)),
+            primary_scales.reshape(row_count, scale_cols),
+        ],
+        axis=1,
+    )
+    notice = jnp.pad(notice, ((0, 0), (0, -notice.shape[1] % TILE)))
+    held = jnp.concatenate([tokens, notice], axis=1)
+    dev_bits = dev_count.bit_length() - 1
+    all_bits = device_count.bit_length() - 1
+    order = list(range(dev_bits))[::-1] + list(range(dev_bits, all_bits))[::-1]
+    for bit in order:
+        pairs = [(device, device ^ 1 << bit) for device in range(device_count)]
+        held = jnp.concatenate([held, lax.ppermute(held, AXES, pairs)], axis=0)
     device_ids = jnp.arange(device_count, dtype=jnp.int32)
-    matched = expert_flat[:, None] == place_all[None, :]
-    has_copy = jnp.any(matched, axis=1)
-    holder = jnp.sum(jnp.where(matched, device_ids[None, :], 0), axis=1)
-    use_copy = (replica.reshape(pair_count) == 1) & has_copy
-    target = jnp.where(use_copy, holder, expert_flat // holding)
-    slot_id = jnp.where(use_copy, holding, expert_flat % holding)
+    my_id = first_dev + my_dev
+    apart = device_ids ^ my_id
+    spot_of = sum((apart >> bit & 1) << step for step, bit in enumerate(order))
+
+    notices = held[:, width_in:].reshape(device_count, row_count, -1)[spot_of]
+    experts_all = notices[:, :, :top_count].astype(jnp.int32).reshape(device_count, pair_count)
+    replica_all = notices[:, :, top_count : 2 * top_count].astype(jnp.int32)
+    replica_all = replica_all.reshape(device_count, pair_count)
+    place_all = notices[:, 0, 2 * top_count].astype(jnp.int32)
+    my_place = new_place[0]
+    owner_notice = lax.dynamic_index_in_dim(notices, my_place // holding, 0, keepdims=False)
+    owner_scales = owner_notice[:, 2 * top_count + 1 : 2 * top_count + 1 + scale_cols]
+    new_scales = lax.dynamic_index_in_dim(
+        owner_scales.reshape(primary_scales.shape), my_place % holding, 0
+    )
+
+    matched = experts_all[:, :, None] == place_all[None, None, :]
+    has_copy = jnp.any(matched, axis=2)
+    holder = jnp.sum(jnp.where(matched, device_ids[None, None, :], 0), axis=2)
+    use_copy = (replica_all == 1) & has_copy
+    target = jnp.where(use_copy, holder, experts_all // holding)
+    slot_id = jnp.where(use_copy, holding, experts_all % holding)
     pair_order = jnp.arange(pair_count)
-    before = pair_order[None, :] < pair_order[:, None]
-    position = jnp.sum((target[:, None] == target[None, :]) & before, axis=1)
+    before = pair_order[:, None] < pair_order[None, :]
+    position = jnp.sum((target[:, :, None] == target[:, None, :]) & before[None], axis=1)
     served = position < CAP
+    arriving = served & (target == my_id)
+    slot_load = jnp.stack(
+        [jnp.sum((arriving & (slot_id == slot)).astype(jnp.int32)) for slot in range(holding + 1)]
+    )[None]
+
     cells = 2 * CAP
-    same_expert = (expert_flat[:, None] == expert_flat[None, :]) & before & served[None, :]
-    cell_index = expert_flat * cells + jnp.sum(same_expert, axis=1)
     cell_count = device_count * holding * cells
-    placed = (cell_index[None, :] == jnp.arange(cell_count)[:, None]) & served[None, :]
-    row_hits = jnp.any(placed.reshape(cell_count, row_count, top_count), axis=2)
-    row_buffer = jnp.dot(row_hits.astype(jnp.bfloat16), tokens, preferred_element_type=jnp.float32)
-    row_buffer = row_buffer.astype(jnp.bfloat16).reshape(device_count, holding * cells, width_in)
-    row_block = lax.all_to_all(row_buffer, AXES, split_axis=0, concat_axis=0, tiled=True)
-
-    dest_hit = (target[None, :] == device_ids[:, None]) & served[None, :]
-    slot_hit = slot_id[:, None] == jnp.arange(holding + 1)[None, :]
-    counted = jnp.dot(
-        dest_hit.astype(jnp.bfloat16),
-        slot_hit.astype(jnp.bfloat16),
-        preferred_element_type=jnp.float32,
-    )
-    counts = lax.all_to_all(
-        counted.astype(jnp.bfloat16), AXES, split_axis=0, concat_axis=0, tiled=True
-    )
-    slot_load = jnp.sum(counts.astype(jnp.float32), axis=0, keepdims=True).astype(jnp.int32)
-
-    activated = serve(row_block.reshape(cell_count, width_in), primary_q, primary_scales)
+    cell = experts_all % holding * cells + use_copy * CAP + position
+    mine = served & (experts_all // holding == my_id)
+    cell_ids = jnp.arange(holding * cells)
+    hit = mine[:, None, :] & (cell[:, None, :] == cell_ids[None, :, None])
+    row_at = spot_of[:, None] * row_count + jnp.sum(
+        jnp.where(hit, pair_order // top_count, 0), axis=2
+    )
+    row_at = jnp.where(jnp.any(hit, axis=2), row_at, -1).reshape(cell_count)
+    row_hits = row_at[:, None] == jnp.arange(device_count * row_count)[None, :]
+    row_block = jnp.dot(row_hits.astype(jnp.bfloat16), held, preferred_element_type=jnp.float32)
+    activated = serve(row_block.astype(jnp.bfloat16), primary_q, primary_scales)
     returned = lax.all_to_all(
         activated.reshape(device_count, holding * cells, hidden),
         AXES,
@@ -219,8 +235,10 @@
         concat_axis=0,
         tiled=True,
     )
+    my_cell = (experts_all // holding * (holding * cells) + cell)[my_id]
+    placed = (my_cell[:, None] == jnp.arange(cell_count)[None, :]) & served[my_id][:, None]
     selected = jnp.dot(
-        placed.T.astype(jnp.bfloat16),
+        placed.astype(jnp.bfloat16),
         returned.reshape(cell_count, hidden),
         preferred_element_type=jnp.float32,
     )
@@ -232,7 +250,7 @@
     dest_side = device_ids % dev_count // half
     source_side = source % dev_count // half
     crossing = source_side != dest_side
-    row_at = (source // dev_count % pooled * half + source % half) * holding + place_all % holding
+    source_row = (source // dev_count % pooled * half + source % half) * holding + place_all % holding
     pool_of = device_ids // dev_count // pooled
     peers = (pool_of[:, None] == pool_of[None, :]) & (dest_side[:, None] == dest_side[None, :])
     ahead = peers & crossing[None, :] & (device_ids[None, :] < device_ids[:, None])
@@ -243,27 +261,31 @@
     leaving = (pool_of == my_pool) & (dest_side != my_side) & crossing
     slots = jnp.arange(POOL)
     leave_rows = jnp.sum(
-        jnp.where(leaving[None, :] & (rank[None, :] == slots[:, None]), row_at[None, :], 0), axis=1
+        jnp.where(leaving[None, :] & (rank[None, :] == slots[:, None]), source_row[None, :], 0), axis=1
     )
     staying = (pool_of == my_pool) & (dest_side == my_side)
     place_in_pool = device_ids // dev_count % pooled * half + device_ids % half
     give_rows = jnp.sum(
         jnp.where(
             staying[None, :] & (place_in_pool[None, :] == slots[:, None]),
-            jnp.where(crossing, POOL * holding + rank, row_at)[None, :],
+            jnp.where(crossing, POOL * holding + rank, source_row)[None, :],
             0,
         ),
         axis=1,
     )
-    pieces = []
+    new_weights = None
+    start = 0
     for block in spread:
         arrived = cross_over(cross_count, gather(leave_rows, block, block), over)
         given = gather(give_rows, block, arrived)
         given = lax.all_to_all(
             given, AXES, split_axis=0, concat_axis=0, tiled=True, axis_index_groups=pools
-        )
-        pieces.append(given.reshape(1, -1, hidden))
-    new_weights = jnp.concatenate(pieces, axis=1)
+        ).reshape(1, -1, hidden)
+        if new_weights is None:
+            new_weights = jnp.pad(given, ((0, 0), (0, width_in - given.shape[1]), (0, 0)))
+        else:
+            new_weights = lax.dynamic_update_slice(new_weights, given, (0, start, 0))
+        start += given.shape[1]
     return (new_weights, new_scales, hidden_out, slot_load)
 
 

time: 884 us -> 498 us (0.56)
  Pallas kernels: 371 us -> 54.9 us
  waiting for transfers between devices: 417 us -> 364 us
  local copies, waits for them, and re-layouts: 36.3 us -> 18.3 us
  other arithmetic: 11.4 us -> 21.6 us
    pallas_call x4, Pallas kernels: 358 us -> 19.2 us  [gather(): pl.pallas_call(functools.partial(gather_kernel, count), in_specs=[pl.Bloc...]
    ppermute x2, waiting for transfers between devices: 250 us -> 197 us  [branch(): got = lax.ppermute(held[:size], AXES, pairs)]
    ppermute x0 -> x5, waiting for transfers between devices: none -> 42.2 us  [per_device(): held = jnp.concatenate([held, lax.ppermute(held, AXES, pairs)], axis=0)]
    all_to_all x5 -> x2, waiting for transfers between devices: 111 us -> 79.2 us  [per_device(): lax.all_to_all(by_chunk(primary_q, start, height), AXES, split_axis=0, co...]
    pallas_call x0 -> x2, Pallas kernels: none -> 22.8 us  [by_chunk(): pl.pallas_call(copy_kernel, grid=(POOL,), in_specs=[pl.BlockSpec((holding...]
    all_to_all x5 -> x2, starting transfers between devices: 22.2 us -> 9.39 us  [per_device(): lax.all_to_all(by_chunk(primary_q, start, height), AXES, split_axis=0, co...]
    reshape x6 -> x3, local copies, waits for them, and re-layouts: 12 us -> 0.23 us  [the longest x1 0.09 us: per_device(): primary_scales.reshape(row_count, scale_cols)]
    slice x3, local copies, waits for them, and re-layouts: 10.4 us -> 1.1 us  [the longest x1 0.91 us: per_device(): notices = held[:, width_in:].reshape(device_count, row_count, -1)[spot_of]]
  transfers between devices with their start and end apart: 10 -> 12, of which waited for: 7 -> 10; matrix products, arithmetic and copies ran while one was open for 4% -> 4% of each run, Pallas kernels for 42% -> 8%
where the time goes in v2:
time: 498 us; the launch traced here: 503 us
  waiting for transfers between devices  364 us (73%)
  Pallas kernels  54.9 us (11%)
  starting transfers between devices  37.5 us (8%)
  other arithmetic  21.6 us (4%)
  local copies, waits for them, and re-layouts  18.3 us (4%)
    ppermute x2, waiting for transfers between devices, branch(): got = lax.ppermute(held[:size], AXES, pairs)  197 us
    all_to_all x2, waiting for transfers between devices, per_device(): lax.all_to_all(by_chunk(primary_q, start, height), AXES, split_axis=0, co...  79.2 us
    ppermute x5, waiting for transfers between devices, per_device(): held = jnp.concatenate([held, lax.ppermute(held, AXES, pairs)], axis=0)  42.2 us
    all_to_all x2, waiting for transfers between devices, per_device(): lax.all_to_all(given, AXES, split_axis=0, concat_axis=0, tiled=True, axis...  40.6 us
    pallas_call x2, Pallas kernels, by_chunk(): pl.pallas_call(copy_kernel, grid=(POOL,), in_specs=[pl.BlockSpec((holding...  22.8 us
    pallas_call x4, Pallas kernels, gather(): pl.pallas_call(functools.partial(gather_kernel, count), in_specs=[pl.Bloc...  19.2 us
    pallas_call x1, Pallas kernels, serve(): pl.pallas_call(expert_kernel, grid=(steps,), in_specs=[pl.BlockSpec((coun...  12.8 us
  transfers between devices with their start and end apart: 12, of which 10 were waited for; matrix products, arithmetic and copies ran while one was open for 4% of the time, Pallas kernels for 8%

profile of v2, /device:TPU:0, one launch (start us, length us, event | category | flops | bytes accessed | tf_op | source)
XLA Modules:
  0.0 503.4 jit_solution(240115622639819839)
XLA Ops:
  2.8 0.8 copy.73
  3.9 1.6 constant_dynamic-update-slice_fusion.4
  5.5 4.0 collective-permute-start.32
  9.5 5.8 %collective-permute-done.32 = bf16[16,3712]{1,0:T(8,128)(2,1)S(1)} collective-permute-done((bf16[16,3712]{1,0:T(8,128)(2,1)S(1)}, bf16[16,3712]{1,0:T(8,128)(2,1)S(1)}, u32[]{:S(2)}, u32[]{:S(2)}) %collective-permute-start.32) | collective-permute-done | bytes 118816 | tf_op jit(solution)/shard_map/ppermute | solution.py:185
  15.3 0.9 pad_maximum_fusion.3
  16.2 0.8 collective-permute-start.33
  17.0 6.2 %collective-permute-done.33 = bf16[32,3712]{1,0:T(8,128)(2,1)S(1)} collective-permute-done((bf16[32,3712]{1,0:T(8,128)(2,1)S(1)}, bf16[32,3712]{1,0:T(8,128)(2,1)S(1)}, u32[]{:S(2)}, u32[]{:S(2)}) %collective-permute-start.33) | collective-permute-done | bytes 237600 | tf_op jit(solution)/shard_map/ppermute | solution.py:185
  23.3 0.9 pad_maximum_fusion.2
  24.2 1.3 collective-permute-start.34
  25.5 9.9 %collective-permute-done.34 = bf16[64,3712]{1,0:T(8,128)(2,1)S(1)} collective-permute-done((bf16[64,3712]{1,0:T(8,128)(2,1)S(1)}, bf16[64,3712]{1,0:T(8,128)(2,1)S(1)}, u32[]{:S(2)}, u32[]{:S(2)}) %collective-permute-start.34) | collective-permute-done | bytes 475168 | tf_op jit(solution)/shard_map/ppermute | solution.py:185
  35.4 1.0 pad_maximum_fusion.1
  36.4 1.4 collective-permute-start.35
  38.5 0.8 constant_dynamic-update-slice_fusion.2
  39.3 1.0 constant_dynamic-update-slice_fusion.1
  40.3 16.6 %collective-permute-done.35 = bf16[128,3712]{1,0:T(8,128)(2,1)S(1)} collective-permute-done((bf16[128,3712]{1,0:T(8,128)(2,1)S(1)}, bf16[128,3712]{1,0:T(8,128)(2,1)S(1)}, u32[]{:S(2)}, u32[]{:S(2)}) %collective-permute-start.35) | collective-permute-done | bytes 950304 | tf_op jit(solution)/shard_map/ppermute | solution.py:185
  56.8 1.4 constant_dynamic-update-slice_fusion
  58.6 3.7 collective-permute-done.36
  62.3 1.4 constant_dynamic-update-slice_fusion.5
  63.7 0.9 slice.112
  69.2 3.3 convolution_convert_fusion.x_ref
  72.5 12.8 %shard_map.108 = bf16[256,1024]{1,0:T(8,128)(2,1)} custom-call(bf16[256,3712]{1,0:T(8,128)(2,1)S(1)} %convolution_convert_fusion.x_ref, bf16[2,3584,1024]{2,1,0:T(8,128)(2,1)} %q_ref.1, f32[2,7,4,1024]{3,2,1,0:T(4,128)S(1)} %reshape_reshape.3.s_ref), custom_call_target="tpu_custom_call" | custom-call | flops 3758096384 | bytes 17039360 | tf_op jit(solution)/shard_map/pallas_call | solution.py:51
  85.2 8.1 %all-to-all-start.4 = ((bf16[32,8,1024]{2,1,0:T(8,128)(2,1)}), bf16[32,8,1024]{2,1,0:T(8,128)(2,1)S(1)}, u32[]{:S(2)}, u32[]{:S(2)}) async-start(bf16[32,8,1024]{2,1,0:T(8,128)(2,1)} %bitcast.13), calls=%async_computation.4 | async-start | bytes 1048576 | tf_op jit(solution)/shard_map/all_to_all | solution.py:231
  93.4 11.4 %shard_map.102 = bf16[16,2,112,1024]{3,2,1,0:T(8,128)(2,1)} custom-call(bf16[2,3584,1024]{2,1,0:T(8,128)(2,1)} %q_ref.1), custom_call_target="tpu_custom_call" | custom-call | tf_op jit(solution)/shard_map/pallas_call | solution.py:112
  104.8 5.0 all-to-all-done.4
  109.7 4.7 all-to-all-start
  114.5 11.4 %shard_map.105 = bf16[16,2,112,1024]{3,2,1,0:T(8,128)(2,1)} custom-call(bf16[2,3584,1024]{2,1,0:T(8,128)(2,1)} %q_ref.1), custom_call_target="tpu_custom_call" | custom-call | tf_op jit(solution)/shard_map/pallas_call | solution.py:112
  125.9 79.2 %all-to-all-done = bf16[16,2,112,1024]{3,2,1,0:T(8,128)(2,1)} async-done(((bf16[16,2,112,1024]{3,2,1,0:T(8,128)(2,1)}), bf16[16,2,112,1024]{3,2,1,0:T(8,128)(2,1)}, u32[]{:S(2)}, u32[]{:S(2)}) %all-to-all-start) | async-done | bytes 7340064 | tf_op jit(solution)/shard_map/all_to_all | solution.py:160
  205.1 4.7 all-to-all-start.2
  212.7 4.9 shard_map.103
  217.6 121.8 %conditional.2 = (bf16[16,112,1024]{2,1,0:T(8,128)(2,1)}) conditional(s32[]{:T(128)} %clamp.4, () %tuple.110, bf16[16,112,1024]{2,1,0:T(8,128)(2,1)} %shard_map.103, bf16[16,112,1024]{2,1,0:T(8,128)(2,1)} %shard_map.103, bf16[16,112,1024]{2,1,0:T(8,128)(2,1)} %shard_map.103, ...), branch_computations={%region_4.5_spmd, %region_5.6_spmd, %region_6.7_spmd, %region_7.8_... | conditional | bytes 27754546 | solution.py:133
  217.6 1.6 slice.77
  219.3 117.6 %collective-permute-done.7 = bf16[8,112,1024]{2,1,0:T(8,128)(2,1)S(1)} collective-permute-done((bf16[8,112,1024]{2,1,0:T(8,128)(2,1)S(1)}, bf16[8,112,1024]{2,1,0:T(8,128)(2,1)S(1)}, u32[]{:S(2)}, u32[]{:S(2)}) %collective-permute-start.7) | collective-permute-done | bytes 1835040 | tf_op jit(solution)/shard_map/cond/branch_8_fun/ppermute | solution.py:128
  336.9 2.4 pad.87
  339.3 4.6 shard_map.104
  343.9 4.5 all-to-all-start.1
  348.5 5.1 %shard_map.106 = bf16[16,112,1024]{2,1,0:T(8,128)(2,1)} custom-call(s32[16]{0:T(128)} %select_reduce_fusion.1.index_ref, bf16[32,112,1024]{2,1,0:T(8,128)(2,1)} %bitcast.5.near_ref.far_ref, bf16[32,112,1024]{2,1,0:T(8,128)(2,1)} %bitcast.5.near_ref.far_ref), custom_call_target="tpu_custom_call" | custom-call | tf_op jit(solution)/shard_map/pallas_call | solution.py:97
  353.6 87.3 %conditional.3 = (bf16[16,112,1024]{2,1,0:T(8,128)(2,1)}) conditional(s32[]{:T(128)} %clamp.4, () %tuple.111, bf16[16,112,1024]{2,1,0:T(8,128)(2,1)} %shard_map.106, bf16[16,112,1024]{2,1,0:T(8,128)(2,1)} %shard_map.106, bf16[16,112,1024]{2,1,0:T(8,128)(2,1)} %shard_map.106, ...), branch_computations={%region_21.22_spmd, %region_22.23_spmd, %region_23.24_spmd, %regio... | conditional | bytes 27754546 | solution.py:133
  353.6 1.6 slice.92
  355.3 3.4 collective-permute-start.23
  358.7 79.8 %collective-permute-done.23 = bf16[8,112,1024]{2,1,0:T(8,128)(2,1)S(1)} collective-permute-done((bf16[8,112,1024]{2,1,0:T(8,128)(2,1)S(1)}, bf16[8,112,1024]{2,1,0:T(8,128)(2,1)S(1)}, u32[]{:S(2)}, u32[]{:S(2)}) %collective-permute-start.23) | collective-permute-done | bytes 1835040 | tf_op jit(solution)/shard_map/cond/branch_8_fun/ppermute | solution.py:128
  438.5 2.4 pad.102
  440.9 4.7 shard_map.107
  445.5 4.5 all-to-all-start.3
  451.5 0.8 convert_reduce_fusion.3
  452.3 2.4 add_bitcast_fusion
  454.7 1.0 fusion.1
  455.7 40.6 %all-to-all-done.3 = bf16[16,112,1024]{2,1,0:T(8,128)(2,1)} async-done(((bf16[16,112,1024]{2,1,0:T(8,128)(2,1)}), bf16[16,112,1024]{2,1,0:T(8,128)(2,1)}, u32[]{:S(2)}, u32[]{:S(2)}) %all-to-all-start.3) | async-done | bytes 3670048 | tf_op jit(solution)/shard_map/all_to_all | solution.py:281
  496.4 7.0 %pad_maximum_fusion = bf16[1,3584,1024]{2,1,0:T(8,128)(2,1)} fusion(bf16[1,1792,1024]{2,1,0:T(8,128)(2,1)} %bitcast.6, bf16[1,1792,1024]{2,1,0:T(8,128)(2,1)} %bitcast.4), kind=kLoop, calls=%fused_computation.1 | loop fusion | flops 14680064 | bytes 14680064 | tf_op jit(solution)/shard_map/dynamic_update_slice | solution.py:287
  (65 shorter events, 11.0 us)
Async XLA Ops:
  5.5 9.8 %collective-permute-start.32 = (bf16[16,3712]{1,0:T(8,128)(2,1)S(1)}, bf16[16,3712]{1,0:T(8,128)(2,1)S(1)}, u32[]{:S(2)}, u32[]{:S(2)}) collective-permute-start(bf16[16,3712]{1,0:T(8,128)(2,1)S(1)} %get-tuple-element.112), channel_id=1, source_target_pairs={{0,4},{1,5},{2,6},{3,7},{4,0},{5,1},{6,2},{7,3},{8,12},{9,13},{10,... | collective-permute-start | bytes 356360 | tf_op jit(solution)/shard_map/ppermute | solution.py:185
  16.2 7.0 %collective-permute-start.33 = (bf16[32,3712]{1,0:T(8,128)(2,1)S(1)}, bf16[32,3712]{1,0:T(8,128)(2,1)S(1)}, u32[]{:S(2)}, u32[]{:S(2)}) collective-permute-start(bf16[32,3712]{1,0:T(8,128)(2,1)S(1)} %pad_maximum_fusion.3), channel_id=1, source_target_pairs={{0,2},{1,3},{2,0},{3,1},{4,6},{5,7},{6,4},{7,5},{8,10},{9,11},{10,... | collective-permute-start | bytes 712712 | tf_op jit(solution)/shard_map/ppermute | solution.py:185
  24.2 34.0 %copy-start = (bf16[2,28,8]{1,2,0:T(8,128)(2,1)S(1)}, bf16[2,28,8]{1,2,0:T(8,128)(2,1)}, u32[]{:S(2)}) copy-start(bf16[2,28,8]{1,2,0:T(8,128)(2,1)} %param.42) | copy-start | bytes 2692
  24.2 11.2 %collective-permute-start.34 = (bf16[64,3712]{1,0:T(8,128)(2,1)S(1)}, bf16[64,3712]{1,0:T(8,128)(2,1)S(1)}, u32[]{:S(2)}, u32[]{:S(2)}) collective-permute-start(bf16[64,3712]{1,0:T(8,128)(2,1)S(1)} %pad_maximum_fusion.2), channel_id=1, source_target_pairs={{0,1},{1,0},{2,3},{3,2},{4,5},{5,4},{6,7},{7,6},{8,9},{9,8},{10,11... | collective-permute-start | bytes 1425416 | tf_op jit(solution)/shard_map/ppermute | solution.py:185
  36.4 20.5 %collective-permute-start.35 = (bf16[128,3712]{1,0:T(8,128)(2,1)S(1)}, bf16[128,3712]{1,0:T(8,128)(2,1)S(1)}, u32[]{:S(2)}, u32[]{:S(2)}) collective-permute-start(bf16[128,3712]{1,0:T(8,128)(2,1)S(1)} %pad_maximum_fusion.1), channel_id=1, source_target_pairs={{0,16},{1,17},{2,18},{3,19},{4,20},{5,21},{6,22},{7,23},{8,24},{9,... | collective-permute-start | bytes 2850824 | tf_op jit(solution)/shard_map/ppermute | solution.py:185
  58.2 4.1 collective-permute-start.36
  85.2 24.5 %all-to-all-start.4 = ((bf16[32,8,1024]{2,1,0:T(8,128)(2,1)}), bf16[32,8,1024]{2,1,0:T(8,128)(2,1)S(1)}, u32[]{:S(2)}, u32[]{:S(2)}) async-start(bf16[32,8,1024]{2,1,0:T(8,128)(2,1)} %bitcast.13), calls=%async_computation.4 | async-start | bytes 1048576 | tf_op jit(solution)/shard_map/all_to_all | solution.py:231
  109.7 95.3 %all-to-all-start = ((bf16[16,2,112,1024]{3,2,1,0:T(8,128)(2,1)}), bf16[16,2,112,1024]{3,2,1,0:T(8,128)(2,1)}, u32[]{:S(2)}, u32[]{:S(2)}) async-start(bf16[16,2,112,1024]{3,2,1,0:T(8,128)(2,1)} %shard_map.102), calls=%async_computation | async-start | bytes 14680064 | tf_op jit(solution)/shard_map/all_to_all | solution.py:160
  205.1 138.9 %all-to-all-start.2 = ((bf16[16,2,112,1024]{3,2,1,0:T(8,128)(2,1)}), bf16[16,2,112,1024]{3,2,1,0:T(8,128)(2,1)}, u32[]{:S(2)}, u32[]{:S(2)}) async-start(bf16[16,2,112,1024]{3,2,1,0:T(8,128)(2,1)} %shard_map.105), calls=%async_computation.2 | async-start | bytes 14680064 | tf_op jit(solution)/shard_map/all_to_all | solution.py:160
  219.2 117.7 %collective-permute-start.7 = (bf16[8,112,1024]{2,1,0:T(8,128)(2,1)S(1)}, bf16[8,112,1024]{2,1,0:T(8,128)(2,1)S(1)}, u32[]{:S(2)}, u32[]{:S(2)}) collective-permute-start(bf16[8,112,1024]{2,1,0:T(8,128)(2,1)S(1)} %slice.77), channel_id=1, source_target_pairs={{0,4},{1,5},{2,6},{3,7},{4,0},{5,1},{6,2},{7,3},{8,12},{9,13},{10,... | collective-permute-start | bytes 5505032 | tf_op jit(solution)/shard_map/cond/branch_8_fun/ppermute | solution.py:128
  343.9 101.6 %all-to-all-start.1 = ((bf16[16,112,1024]{2,1,0:T(8,128)(2,1)}), bf16[16,112,1024]{2,1,0:T(8,128)(2,1)}, u32[]{:S(2)}, u32[]{:S(2)}) async-start(bf16[16,112,1024]{2,1,0:T(8,128)(2,1)} %shard_map.104), calls=%async_computation.1 | async-start | bytes 7340032 | tf_op jit(solution)/shard_map/all_to_all | solution.py:281
  355.3 83.2 %collective-permute-start.23 = (bf16[8,112,1024]{2,1,0:T(8,128)(2,1)S(1)}, bf16[8,112,1024]{2,1,0:T(8,128)(2,1)S(1)}, u32[]{:S(2)}, u32[]{:S(2)}) collective-permute-start(bf16[8,112,1024]{2,1,0:T(8,128)(2,1)S(1)} %slice.92), channel_id=1, source_target_pairs={{0,4},{1,5},{2,6},{3,7},{4,0},{5,1},{6,2},{7,3},{8,12},{9,13},{10,... | collective-permute-start | bytes 5505032 | tf_op jit(solution)/shard_map/cond/branch_8_fun/ppermute | solution.py:128
  445.5 4.6 copy-start.1
  445.5 50.8 %all-to-all-start.3 = ((bf16[16,112,1024]{2,1,0:T(8,128)(2,1)}), bf16[16,112,1024]{2,1,0:T(8,128)(2,1)}, u32[]{:S(2)}, u32[]{:S(2)}) async-start(bf16[16,112,1024]{2,1,0:T(8,128)(2,1)} %shard_map.107), calls=%async_computation.3 | async-start | bytes 7340032 | tf_op jit(solution)/shard_map/all_to_all | solution.py:281

commit v3 on v2

--- a/solution.py
+++ b/solution.py
@@ -10,6 +10,7 @@
 TILE = 128
 CAP = 2
 POOL = 16
+VMEM_LIMIT = 60 * 1024 * 1024
 AXES = ("group", "dev")
 PARTS = (112, 112)
 
@@ -59,7 +60,7 @@
         out_specs=pl.BlockSpec((count, hidden), lambda k: (0, 0)),
         out_shape=jax.ShapeDtypeStruct((count, hidden), jnp.bfloat16),
         scratch_shapes=[pltpu.VMEM((count, hidden), jnp.float32)],
-        compiler_params=pltpu.CompilerParams(vmem_limit_bytes=48 * 1024 * 1024),
+        compiler_params=pltpu.CompilerParams(vmem_limit_bytes=VMEM_LIMIT),
         cost_estimate=pl.CostEstimate(
             flops=2 * count * width_in * hidden * holding,
             bytes_accessed=2 * (values.size + count * (width_in + hidden)),
@@ -68,69 +69,135 @@
     )(rows, values, wide)
 
 
-def gather_kernel(count, index_ref, near_ref, far_ref, out_ref, sem):
+def through_vmem(count, sources, out_at, held, in_sem, out_sem):
+    def leave(spot):
+        pltpu.make_async_copy(held.at[spot], held.at[spot], in_sem.at[spot]).wait()
+        pltpu.make_async_copy(held.at[spot], out_at(spot), out_sem.at[spot]).start()
+
+    def finish(spot):
+        pltpu.make_async_copy(held.at[spot], out_at(spot), out_sem.at[spot]).wait()
+
+    for stage in (sources, leave, finish):
+        pl.loop(0, count)(stage)
+
+
+def gather_kernel(index_ref, near_ref, far_ref, out_ref, held, in_sem, out_sem):
     near_count = near_ref.shape[0]
 
-    def step(spot, carry):
+    def start(spot):
         index = index_ref[spot]
 
         @pl.when(index < near_count)
         def _():
-            pltpu.make_async_copy(
-                near_ref.at[jnp.minimum(index, near_count - 1)], out_ref.at[spot], sem
-            ).start()
+            near_index = jnp.minimum(index, near_count - 1)
+            pltpu.make_async_copy(near_ref.at[near_index], held.at[spot], in_sem.at[spot]).start()
 
         @pl.when(index >= near_count)
         def _():
-            far_index = jnp.maximum(index - near_count, 0)
-            pltpu.make_async_copy(far_ref.at[far_index], out_ref.at[spot], sem).start()
-
-        return carry
-
-    lax.fori_loop(0, count, step, 0)
-    pltpu.make_async_copy(out_ref, out_ref, sem).wait()
+            far_index = jnp.clip(index - near_count, 0, far_ref.shape[0] - 1)
+            pltpu.make_async_copy(far_ref.at[far_index], held.at[spot], in_sem.at[spot]).start()
+
+    through_vmem(out_ref.shape[0], start, lambda spot: out_ref.at[spot], held, in_sem, out_sem)
 
 
 def gather(indices, near, far):
     count = indices.shape[0]
     anywhere = pl.BlockSpec(memory_space=pl.ANY)
+    out = jax.ShapeDtypeStruct((count,) + near.shape[1:], near.dtype)
     return pl.pallas_call(
-        functools.partial(gather_kernel, count),
+        gather_kernel,
         in_specs=[pl.BlockSpec(memory_space=pltpu.SMEM), anywhere, anywhere],
-        out_specs=pl.BlockSpec(memory_space=pltpu.VMEM),
-        out_shape=jax.ShapeDtypeStruct((count,) + near.shape[1:], near.dtype),
-        scratch_shapes=[pltpu.SemaphoreType.DMA],
+        out_specs=anywhere,
+        out_shape=out,
+        scratch_shapes=[
+            pltpu.VMEM(out.shape, out.dtype),
+            pltpu.SemaphoreType.DMA((count,)),
+            pltpu.SemaphoreType.DMA((count,)),
+        ],
+        compiler_params=pltpu.CompilerParams(vmem_limit_bytes=VMEM_LIMIT),
+        cost_estimate=pl.CostEstimate(
+            flops=0, bytes_accessed=4 * out.size, transcendentals=0
+        ),
     )(indices, near, far)
 
 
-def copy_kernel(in_ref, out_ref):
-    out_ref[0] = in_ref[...]
+def chunk_kernel(first, in_ref, out_ref, held, in_sem, out_sem):
+    height = out_ref.shape[2]
+
+    def start(spot):
+        pltpu.make_async_copy(
+            in_ref.at[:, pl.ds(first + spot * height, height), :], held.at[spot], in_sem.at[spot]
+        ).start()
+
+    through_vmem(POOL, start, lambda spot: out_ref.at[spot], held, in_sem, out_sem)
 
 
 def by_chunk(values, first, height):
     holding, _, hidden = values.shape
+    anywhere = pl.BlockSpec(memory_space=pl.ANY)
+    out = jax.ShapeDtypeStruct((POOL, holding, height, hidden), values.dtype)
     return pl.pallas_call(
-        copy_kernel,
-        grid=(POOL,),
-        in_specs=[pl.BlockSpec((holding, height, hidden), lambda k: (0, first // height + k, 0))],
-        out_specs=pl.BlockSpec((1, holding, height, hidden), lambda k: (k, 0, 0, 0)),
-        out_shape=jax.ShapeDtypeStruct((POOL, holding, height, hidden), values.dtype),
+        functools.partial(chunk_kernel, first),
+        in_specs=[anywhere],
+        out_specs=anywhere,
+        out_shape=out,
+        scratch_shapes=[
+            pltpu.VMEM(out.shape, out.dtype),
+            pltpu.SemaphoreType.DMA((POOL,)),
+            pltpu.SemaphoreType.DMA((POOL,)),
+        ],
+        compiler_params=pltpu.CompilerParams(vmem_limit_bytes=VMEM_LIMIT),
+        cost_estimate=pl.CostEstimate(
+            flops=0, bytes_accessed=4 * out.size, transcendentals=0
+        ),
     )(values)
 
 
-def cross_over(count, blocks, pairs):
-    most = blocks.shape[0]
-
+def join_kernel(first, blocks_ref, *refs):
+    out_ref, held, in_sem, out_sem = refs[-4:]
+    count, height, _ = blocks_ref.shape
+
+    def start(spot):
+        pltpu.make_async_copy(blocks_ref.at[spot], held.at[spot], in_sem.at[spot]).start()
+
+    def out_at(spot):
+        return out_ref.at[0, pl.ds(first + spot * height, height), :]
+
+    through_vmem(count, start, out_at, held, in_sem, out_sem)
+
+
+def join(weights, blocks, first, width_in):
+    count, _, hidden = blocks.shape
+    anywhere = pl.BlockSpec(memory_space=pl.ANY)
+    operands = (blocks,) if weights is None else (blocks, weights)
+    return pl.pallas_call(
+        functools.partial(join_kernel, first),
+        in_specs=[anywhere] * len(operands),
+        out_specs=anywhere,
+        out_shape=jax.ShapeDtypeStruct((1, width_in, hidden), blocks.dtype),
+        input_output_aliases={} if weights is None else {1: 0},
+        scratch_shapes=[
+            pltpu.VMEM(blocks.shape, blocks.dtype),
+            pltpu.SemaphoreType.DMA((count,)),
+            pltpu.SemaphoreType.DMA((count,)),
+        ],
+        compiler_params=pltpu.CompilerParams(vmem_limit_bytes=VMEM_LIMIT),
+        cost_estimate=pl.CostEstimate(flops=0, bytes_accessed=4 * blocks.size, transcendentals=0),
+    )(*operands)
+
+
+def cross_over(count, leave_rows, give_rows, block, pairs):
     def branch_of(size):
-        def branch(held):
+        def branch(leave_rows, give_rows, block):
             if size == 0:
-                return jnp.zeros_like(held)
-            got = lax.ppermute(held[:size], AXES, pairs)
-            return jnp.pad(got, ((0, most - size), (0, 0), (0, 0)))
+                return gather(give_rows, block, block)
+            arrived = lax.ppermute(gather(leave_rows[:size], block, block), AXES, pairs)
+            return gather(give_rows, block, arrived)
 
         return branch
 
-    return lax.switch(count, [branch_of(size) for size in range(most + 1)], blocks)
+    branches = [branch_of(size) for size in range(POOL + 1)]
+    return lax.switch(count, branches, leave_rows, give_rows, block)
 
 
 def per_device(primary_q, primary_scales, new_place, tokens, experts, replica, route_num):
@@ -228,24 +295,19 @@
     row_hits = row_at[:, None] == jnp.arange(device_count * row_count)[None, :]
     row_block = jnp.dot(row_hits.astype(jnp.bfloat16), held, preferred_element_type=jnp.float32)
     activated = serve(row_block.astype(jnp.bfloat16), primary_q, primary_scales)
-    returned = lax.all_to_all(
-        activated.reshape(device_count, holding * cells, hidden),
-        AXES,
-        split_axis=0,
-        concat_axis=0,
-        tiled=True,
-    )
+
+    def send_back(*after):
+        blocks, *_ = lax.optimization_barrier((activated, *after))
+        return lax.all_to_all(
+            blocks.reshape(device_count, holding * cells, hidden),
+            AXES,
+            split_axis=0,
+            concat_axis=0,
+            tiled=True,
+        )
+
     my_cell = (experts_all // holding * (holding * cells) + cell)[my_id]
     placed = (my_cell[:, None] == jnp.arange(cell_count)[None, :]) & served[my_id][:, None]
-    selected = jnp.dot(
-        placed.astype(jnp.bfloat16),
-        returned.reshape(cell_count, hidden),
-        preferred_element_type=jnp.float32,
-    )
-    weight = route_num.reshape(pair_count).astype(jnp.float32) / 16.0
-    hidden_out = (selected * weight[:, None]).astype(jnp.bfloat16)
-    hidden_out = hidden_out.reshape(row_count, top_count, hidden)
-
     source = place_all // holding
     dest_side = device_ids % dev_count // half
     source_side = source % dev_count // half
@@ -273,19 +335,29 @@
         ),
         axis=1,
     )
+    given = []
+    for block in spread:
+        given.append(cross_over(cross_count, leave_rows, give_rows, block, over))
+        if len(given) == 1:
+            returned = send_back(given[0], spread[-1])
+            given[0], returned = lax.optimization_barrier((given[0], returned))
     new_weights = None
     start = 0
-    for block in spread:
-        arrived = cross_over(cross_count, gather(leave_rows, block, block), over)
-        given = gather(give_rows, block, arrived)
-        given = lax.all_to_all(
-            given, AXES, split_axis=0, concat_axis=0, tiled=True, axis_index_groups=pools
-        ).reshape(1, -1, hidden)
-        if new_weights is None:
-            new_weights = jnp.pad(given, ((0, 0), (0, width_in - given.shape[1]), (0, 0)))
-        else:
-            new_weights = lax.dynamic_update_slice(new_weights, given, (0, start, 0))
-        start += given.shape[1]
+    for block in given:
+        block = lax.all_to_all(
+            block, AXES, split_axis=0, concat_axis=0, tiled=True, axis_index_groups=pools
+        )
+        new_weights = join(new_weights, block, start, width_in)
+        start += block.shape[0] * block.shape[1]
+
+    selected = jnp.dot(
+        placed.astype(jnp.bfloat16),
+        returned.reshape(cell_count, hidden),
+        preferred_element_type=jnp.float32,
+    )
+    weight = route_num.reshape(pair_count).astype(jnp.float32) / 16.0
+    hidden_out = (selected * weight[:, None]).astype(jnp.bfloat16)
+    hidden_out = hidden_out.reshape(row_count, top_count, hidden)
     return (new_weights, new_scales, hidden_out, slot_load)
 
 

time: 498 us -> 567 us (1.14); the launches traced: 503 us -> 556 us
  waiting for transfers between devices: 364 us -> 427 us
  blocking collectives: 0 us -> 19.7 us
  other arithmetic: 21.6 us -> 10 us
  Pallas kernels: 54.9 us -> 47.3 us
  starting transfers between devices: 37.5 us -> 30 us
    ppermute x5, waiting for transfers between devices: 42.2 us -> 123 us  [per_device(): held = jnp.concatenate([held, lax.ppermute(held, AXES, pairs)], axis=0)]
    all_to_all x0 -> x1, blocking collectives: none -> 19.7 us  [send_back(): lax.all_to_all(blocks.reshape(device_count, holding * cells, hidden), AXE...]
    ppermute x2, waiting for transfers between devices: 197 us -> 184 us  [branch(): arrived = lax.ppermute(gather(leave_rows[:size], block, block), AXES, pairs)]
    all_to_all x3 -> x2, waiting for transfers between devices: 45.6 us -> 35.3 us  [per_device(): lax.all_to_all(block, AXES, split_axis=0, concat_axis=0, tiled=True, axis...]
    all_to_all x3 -> x2, starting transfers between devices: 17.2 us -> 9.39 us  [per_device(): lax.all_to_all(block, AXES, split_axis=0, concat_axis=0, tiled=True, axis...]
    pallas_call x6 -> x8, Pallas kernels: 42.1 us -> 34.3 us  [the longest x4 14.8 us: gather(): pl.pallas_call(gather_kernel, in_specs=[pl.BlockSpec(memory_space=pltpu.S...]
    dynamic_update_slice x1 -> x0, other arithmetic: 7.05 us -> none  [per_device(): new_weights = lax.dynamic_update_slice(new_weights, given, (0, start, 0))]
  transfers between devices with their start and end apart: 12 -> 11, of which waited for: 10 -> 9; matrix products, arithmetic and copies ran while one was open for 4% -> 5% of each run, Pallas kernels for 8% -> 7%
where the time goes in v3:
time: 567 us; the launch traced here: 556 us
  waiting for transfers between devices  427 us (75%)
  Pallas kernels  47.3 us (8%)
  starting transfers between devices  30 us (5%)
  blocking collectives  19.7 us (3%)
  local copies, waits for them, and re-layouts  13.7 us (2%)
  other arithmetic  10 us (2%)
    ppermute x2, waiting for transfers between devices, branch(): arrived = lax.ppermute(gather(leave_rows[:size], block, block), AXES, pairs)  184 us
    ppermute x5, waiting for transfers between devices, per_device(): held = jnp.concatenate([held, lax.ppermute(held, AXES, pairs)], axis=0)  123 us
    all_to_all x2, waiting for transfers between devices, per_device(): lax.all_to_all(by_chunk(primary_q, start, height), AXES, split_axis=0, co...  84.7 us
    all_to_all x2, waiting for transfers between devices, per_device(): lax.all_to_all(block, AXES, split_axis=0, concat_axis=0, tiled=True, axis...  35.3 us
    all_to_all x1, blocking collectives, send_back(): lax.all_to_all(blocks.reshape(device_count, holding * cells, hidden), AXE...  19.7 us
    pallas_call x4, Pallas kernels, gather(): pl.pallas_call(gather_kernel, in_specs=[pl.BlockSpec(memory_space=pltpu.S...  14.8 us
    pallas_call x1, Pallas kernels, serve(): pl.pallas_call(expert_kernel, grid=(steps,), in_specs=[pl.BlockSpec((coun...  13 us
    pallas_call x2, Pallas kernels, by_chunk(): pl.pallas_call(functools.partial(chunk_kernel, first), in_specs=[anywhere...  12 us
  transfers between devices with their start and end apart: 11, of which 9 were waited for; matrix products, arithmetic and copies ran while one was open for 5% of the time, Pallas kernels for 7%

profile of v3, /device:TPU:0, one launch (start us, length us, event | category | flops | bytes accessed | tf_op | source)
XLA Modules:
  0.0 556.1 jit_solution(19856485239623759)
XLA Ops:
  0.6 6.0 %shard_map.103 = bf16[16,2,112,1024]{3,2,1,0:T(8,128)(2,1)} custom-call(bf16[2,3584,1024]{2,1,0:T(8,128)(2,1)} %q_ref.1), custom_call_target="tpu_custom_call" | custom-call | bytes 14680064 | tf_op jit(solution)/shard_map/pallas_call | solution.py:139
  6.7 6.3 %all-to-all-start.2 = ((bf16[16,2,112,1024]{3,2,1,0:T(8,128)(2,1)}), bf16[16,2,112,1024]{3,2,1,0:T(8,128)(2,1)}, u32[]{:S(2)}, u32[]{:S(2)}) async-start(bf16[16,2,112,1024]{3,2,1,0:T(8,128)(2,1)} %shard_map.103), calls=%async_computation.2 | async-start | bytes 14680064 | tf_op jit(solution)/shard_map/all_to_all | solution.py:227
  13.0 6.0 %shard_map.102 = bf16[16,2,112,1024]{3,2,1,0:T(8,128)(2,1)} custom-call(bf16[2,3584,1024]{2,1,0:T(8,128)(2,1)} %q_ref.1), custom_call_target="tpu_custom_call" | custom-call | bytes 14680064 | tf_op jit(solution)/shard_map/pallas_call | solution.py:139
  19.0 84.7 %all-to-all-done.2 = bf16[16,2,112,1024]{3,2,1,0:T(8,128)(2,1)} async-done(((bf16[16,2,112,1024]{3,2,1,0:T(8,128)(2,1)}), bf16[16,2,112,1024]{3,2,1,0:T(8,128)(2,1)}, u32[]{:S(2)}, u32[]{:S(2)}) %all-to-all-start.2) | async-done | bytes 7340064 | tf_op jit(solution)/shard_map/all_to_all | solution.py:227
  103.7 4.7 all-to-all-start
  109.7 0.7 constant_dynamic-update-slice_fusion.4
  110.4 2.6 collective-permute-start.32
  113.0 85.8 %collective-permute-done.32 = bf16[16,3712]{1,0:T(8,128)(2,1)S(1)} collective-permute-done((bf16[16,3712]{1,0:T(8,128)(2,1)S(1)}, bf16[16,3712]{1,0:T(8,128)(2,1)S(1)}, u32[]{:S(2)}, u32[]{:S(2)}) %collective-permute-start.32) | collective-permute-done | bytes 118816 | tf_op jit(solution)/shard_map/ppermute | solution.py:252
  198.9 4.5 collective-permute-start.33
  203.3 5.6 %collective-permute-done.33 = bf16[32,3712]{1,0:T(8,128)(2,1)S(1)} collective-permute-done((bf16[32,3712]{1,0:T(8,128)(2,1)S(1)}, bf16[32,3712]{1,0:T(8,128)(2,1)S(1)}, u32[]{:S(2)}, u32[]{:S(2)}) %collective-permute-start.33) | collective-permute-done | bytes 237600 | tf_op jit(solution)/shard_map/ppermute | solution.py:252
  209.1 11.8 %collective-permute-done.34 = bf16[64,3712]{1,0:T(8,128)(2,1)S(1)} collective-permute-done((bf16[64,3712]{1,0:T(8,128)(2,1)S(1)}, bf16[64,3712]{1,0:T(8,128)(2,1)S(1)}, u32[]{:S(2)}, u32[]{:S(2)}) %collective-permute-start.34) | collective-permute-done | bytes 475168 | tf_op jit(solution)/shard_map/ppermute | solution.py:252
  221.0 1.6 collective-permute-start.35
  222.5 0.7 constant_dynamic-update-slice_fusion.3
  223.3 0.8 constant_dynamic-update-slice_fusion.2
  224.1 1.0 constant_dynamic-update-slice_fusion.1
  225.2 17.0 %collective-permute-done.35 = bf16[128,3712]{1,0:T(8,128)(2,1)S(1)} collective-permute-done((bf16[128,3712]{1,0:T(8,128)(2,1)S(1)}, bf16[128,3712]{1,0:T(8,128)(2,1)S(1)}, u32[]{:S(2)}, u32[]{:S(2)}) %collective-permute-start.35) | collective-permute-done | bytes 950304 | tf_op jit(solution)/shard_map/ppermute | solution.py:252
  242.1 1.4 constant_dynamic-update-slice_fusion
  243.7 0.8 reshape_reshape.3.s_ref
  244.6 3.0 collective-permute-done.36
  247.6 1.4 constant_dynamic-update-slice_fusion.5
  249.0 0.9 slice.112
  251.2 0.7 fusion.22
  252.3 0.7 convert_reduce_fusion
  256.9 4.6 convolution_convert_fusion.x_ref
  261.4 13.0 %shard_map.104 = bf16[256,1024]{1,0:T(8,128)(2,1)} custom-call(bf16[256,3712]{1,0:T(8,128)(2,1)} %convolution_convert_fusion.x_ref, bf16[2,3584,1024]{2,1,0:T(8,128)(2,1)} %q_ref.1, f32[2,7,4,1024]{3,2,1,0:T(4,128)} %reshape_reshape.3.s_ref), custom_call_target="tpu_custom_call" | custom-call | flops 3758096384 | bytes 17039360 | tf_op jit(solution)/shard_map/pallas_call | solution.py:52
  274.5 101.1 %conditional.3 = (bf16[16,112,1024]{2,1,0:T(8,128)(2,1)}) conditional(s32[]{:T(128)} %clamp.4, (s32[16]{0:T(128)S(1)}, bf16[32,112,1024]{2,1,0:T(8,128)(2,1)}) %tuple.114, (s32[16]{0:T(128)S(1)}, bf16[32,112,1024]{2,1,0:T(8,128)(2,1)}, s32[16]{0:T(128)S(1)}) %tuple.115, (s32[16]{0:T(128)S(1)}, ...), branch_computations={%region_21.22_spmd, %region_22.23_spmd, %region_23.24_spmd, %regio... | conditional | bytes 44040268 | solution.py:200
  274.5 3.1 branch_9_fun.6
  277.6 0.7 collective-permute-start.24
  278.4 91.6 %collective-permute-done.24.far_ref = bf16[9,112,1024]{2,1,0:T(8,128)(2,1)S(1)} collective-permute-done((bf16[9,112,1024]{2,1,0:T(8,128)(2,1)}, bf16[9,112,1024]{2,1,0:T(8,128)(2,1)S(1)}, u32[]{:S(2)}, u32[]{:S(2)}) %collective-permute-start.24) | collective-permute-done | bytes 2064416 | tf_op jit(solution)/shard_map/cond/branch_9_fun/ppermute | solution.py:194
  370.0 1.3 copy-done.15
  371.3 4.3 branch_9_fun.7
  375.7 19.7 %all_to_all.25 = bf16[32,8,1024]{2,1,0:T(8,128)(2,1)} all-to-all(bf16[32,8,1024]{2,1,0:T(8,128)(2,1)} %bitcast.79), channel_id=1, replica_groups=mesh['group'=4,'dev'=8] {'group','dev'}, dimensions={0} | all-to-all | bytes 1048576 | tf_op jit(solution)/shard_map/all_to_all | solution.py:301
  395.3 4.7 all-to-all-start.4
  400.1 101.1 %conditional.2 = (bf16[16,112,1024]{2,1,0:T(8,128)(2,1)}) conditional(s32[]{:T(128)} %clamp.4, (s32[16]{0:T(128)S(1)}, bf16[32,112,1024]{2,1,0:T(8,128)(2,1)}) %tuple.112, (s32[16]{0:T(128)S(1)}, bf16[32,112,1024]{2,1,0:T(8,128)(2,1)}, s32[16]{0:T(128)S(1)}) %tuple.113, (s32[16]{0:T(128)S(1)}, ...), branch_computations={%region_4.5_spmd, %region_5.6_spmd, %region_6.7_spmd, %region_7.8_... | conditional | bytes 44040268 | solution.py:200
  400.1 3.1 branch_9_fun.4
  403.2 92.3 %collective-permute-done.8.far_ref = bf16[9,112,1024]{2,1,0:T(8,128)(2,1)S(1)} collective-permute-done((bf16[9,112,1024]{2,1,0:T(8,128)(2,1)}, bf16[9,112,1024]{2,1,0:T(8,128)(2,1)S(1)}, u32[]{:S(2)}, u32[]{:S(2)}) %collective-permute-start.8) | collective-permute-done | bytes 2064416 | tf_op jit(solution)/shard_map/cond/branch_9_fun/ppermute | solution.py:194
  495.5 1.3 copy-done.16
  496.8 4.3 branch_9_fun.5
  501.3 4.7 all-to-all-start.1
  506.5 0.7 dynamic-slice_bitcast_fusion
  507.4 0.7 copy.90
  508.1 0.7 fusion.38
  508.8 0.8 convert_reduce_fusion.3
  509.6 2.5 add_bitcast_fusion
  512.2 1.0 fusion.1
  513.1 3.8 shard_map.105.refs_0_
  516.9 35.3 %all-to-all-done.1.blocks_ref = bf16[16,112,1024]{2,1,0:T(8,128)(2,1)} async-done(((bf16[16,112,1024]{2,1,0:T(8,128)(2,1)}), bf16[16,112,1024]{2,1,0:T(8,128)(2,1)}, u32[]{:S(2)}, u32[]{:S(2)}) %all-to-all-start.1) | async-done | bytes 3670048 | tf_op jit(solution)/shard_map/all_to_all | solution.py:347
  552.2 3.8 shard_map.106
  (97 shorter events, 6.6 us)
Async XLA Ops:
  6.7 97.1 %all-to-all-start.2 = ((bf16[16,2,112,1024]{3,2,1,0:T(8,128)(2,1)}), bf16[16,2,112,1024]{3,2,1,0:T(8,128)(2,1)}, u32[]{:S(2)}, u32[]{:S(2)}) async-start(bf16[16,2,112,1024]{3,2,1,0:T(8,128)(2,1)} %shard_map.103), calls=%async_computation.2 | async-start | bytes 14680064 | tf_op jit(solution)/shard_map/all_to_all | solution.py:227
  19.0 90.1 %copy-start.45 = (bf16[2,28,8]{1,2,0:T(8,128)(2,1)S(1)}, bf16[2,28,8]{1,2,0:T(8,128)(2,1)}, u32[]{:S(2)}) copy-start(bf16[2,28,8]{1,2,0:T(8,128)(2,1)} %param.42) | copy-start | bytes 2692
  19.0 90.3 %copy-start.47 = (s32[16,8]{0,1:T(8,128)S(1)}, s32[16,8]{0,1:T(8,128)}, u32[]{:S(2)}) copy-start(s32[16,8]{0,1:T(8,128)} %param.45) | copy-start | bytes 1540
  19.0 90.4 %copy-start.48 = (s32[16,8]{0,1:T(8,128)S(1)}, s32[16,8]{0,1:T(8,128)}, u32[]{:S(2)}) copy-start(s32[16,8]{0,1:T(8,128)} %param.46) | copy-start | bytes 1540
  19.0 90.6 %copy-start.19 = (bf16[16,3584]{1,0:T(8,128)(2,1)S(1)}, bf16[16,3584]{1,0:T(8,128)(2,1)}, u32[]{:S(2)}) copy-start(bf16[16,3584]{1,0:T(8,128)(2,1)} %param.44) | copy-start | bytes 344068
  103.7 271.9 %all-to-all-start = ((bf16[16,2,112,1024]{3,2,1,0:T(8,128)(2,1)}), bf16[16,2,112,1024]{3,2,1,0:T(8,128)(2,1)}, u32[]{:S(2)}, u32[]{:S(2)}) async-start(bf16[16,2,112,1024]{3,2,1,0:T(8,128)(2,1)} %shard_map.102), calls=%async_computation | async-start | bytes 14680064 | tf_op jit(solution)/shard_map/all_to_all | solution.py:227
  110.4 88.4 %collective-permute-start.32 = (bf16[16,3712]{1,0:T(8,128)(2,1)S(1)}, bf16[16,3712]{1,0:T(8,128)(2,1)S(1)}, u32[]{:S(2)}, u32[]{:S(2)}) collective-permute-start(bf16[16,3712]{1,0:T(8,128)(2,1)S(1)} %get-tuple-element.386), channel_id=1, source_target_pairs={{0,4},{1,5},{2,6},{3,7},{4,0},{5,1},{6,2},{7,3},{8,12},{9,13},{10,... | collective-permute-start | bytes 356360 | tf_op jit(solution)/shard_map/ppermute | solution.py:252
  198.9 10.1 %collective-permute-start.33 = (bf16[32,3712]{1,0:T(8,128)(2,1)S(1)}, bf16[32,3712]{1,0:T(8,128)(2,1)S(1)}, u32[]{:S(2)}, u32[]{:S(2)}) collective-permute-start(bf16[32,3712]{1,0:T(8,128)(2,1)S(1)} %pad_maximum_fusion.2), channel_id=1, source_target_pairs={{0,2},{1,3},{2,0},{3,1},{4,6},{5,7},{6,4},{7,5},{8,10},{9,11},{10,... | collective-permute-start | bytes 712712 | tf_op jit(solution)/shard_map/ppermute | solution.py:252
  209.0 11.9 %collective-permute-start.34 = (bf16[64,3712]{1,0:T(8,128)(2,1)S(1)}, bf16[64,3712]{1,0:T(8,128)(2,1)S(1)}, u32[]{:S(2)}, u32[]{:S(2)}) collective-permute-start(bf16[64,3712]{1,0:T(8,128)(2,1)S(1)} %pad_maximum_fusion.1), channel_id=1, source_target_pairs={{0,1},{1,0},{2,3},{3,2},{4,5},{5,4},{6,7},{7,6},{8,9},{9,8},{10,11... | collective-permute-start | bytes 1425416 | tf_op jit(solution)/shard_map/ppermute | solution.py:252
  221.0 21.2 %collective-permute-start.35 = (bf16[128,3712]{1,0:T(8,128)(2,1)S(1)}, bf16[128,3712]{1,0:T(8,128)(2,1)S(1)}, u32[]{:S(2)}, u32[]{:S(2)}) collective-permute-start(bf16[128,3712]{1,0:T(8,128)(2,1)S(1)} %pad_maximum_fusion), channel_id=1, source_target_pairs={{0,16},{1,17},{2,18},{3,19},{4,20},{5,21},{6,22},{7,23},{8,24},{9,... | collective-permute-start | bytes 2850824 | tf_op jit(solution)/shard_map/ppermute | solution.py:252
  243.5 4.1 collective-permute-start.36
  250.5 10.9 %copy-start.24 = (bf16[32,16,128]{2,1,0:T(8,128)(2,1)}, bf16[32,16,128]{2,1,0:T(8,128)(2,1)S(1)}, u32[]{:S(2)}) copy-start(bf16[32,16,128]{2,1,0:T(8,128)(2,1)S(1)} %gather_fusion) | copy-start | bytes 393220
  250.8 23.7 %copy-start.33 = (bf16[32,16,8]{0,2,1:T(8,128)(2,1)}, bf16[32,16,8]{0,2,1:T(8,128)(2,1)S(1)}, u32[]{:S(2)}) copy-start(bf16[32,16,8]{0,2,1:T(8,128)(2,1)S(1)} %copy.92) | copy-start | bytes 24580
  251.1 23.4 %copy-start.35 = (bf16[32,16,8]{0,2,1:T(8,128)(2,1)}, bf16[32,16,8]{0,2,1:T(8,128)(2,1)S(1)}, u32[]{:S(2)}) copy-start(bf16[32,16,8]{0,2,1:T(8,128)(2,1)S(1)} %copy.91) | copy-start | bytes 24580
  252.1 22.4 %copy-start.43 = (pred[32,128]{1,0:T(8,128)(4,1)}, pred[32,128]{1,0:T(8,128)(4,1)S(1)}, u32[]{:S(2)}) copy-start(pred[32,128]{1,0:T(8,128)(4,1)S(1)} %compare_reduce_fusion) | copy-start | bytes 12292
  252.3 0.8 copy-start.40
  252.3 22.1 %copy-start.42 = (s32[32,128]{1,0:T(8,128)}, s32[32,128]{1,0:T(8,128)S(1)}, u32[]{:S(2)}) copy-start(s32[32,128]{1,0:T(8,128)S(1)} %get-tuple-element.368) | copy-start | bytes 49156
  253.7 20.8 %copy-start.39 = (s32[32,128]{1,0:T(8,128)}, s32[32,128]{1,0:T(8,128)S(1)}, u32[]{:S(2)}) copy-start(s32[32,128]{1,0:T(8,128)S(1)} %fusion.21) | copy-start | bytes 49156
  277.6 92.4 %collective-permute-start.24 = (bf16[9,112,1024]{2,1,0:T(8,128)(2,1)}, bf16[9,112,1024]{2,1,0:T(8,128)(2,1)S(1)}, u32[]{:S(2)}, u32[]{:S(2)}) collective-permute-start(bf16[9,112,1024]{2,1,0:T(8,128)(2,1)} %branch_9_fun.6), channel_id=1, source_target_pairs={{0,4},{1,5},{2,6},{3,7},{4,0},{5,1},{6,2},{7,3},{8,12},{9,13},{10,... | collective-permute-start | bytes 6193160 | tf_op jit(solution)/shard_map/cond/branch_9_fun/ppermute | solution.py:194
  370.0 1.3 copy-start.15
  395.3 105.9 %all-to-all-start.4 = ((bf16[16,112,1024]{2,1,0:T(8,128)(2,1)}), bf16[16,112,1024]{2,1,0:T(8,128)(2,1)}, u32[]{:S(2)}, u32[]{:S(2)}) async-start(bf16[16,112,1024]{2,1,0:T(8,128)(2,1)} %get-tuple-element.391), calls=%async_computation.4 | async-start | bytes 7340032 | tf_op jit(solution)/shard_map/all_to_all | solution.py:347
  403.2 92.4 %collective-permute-start.8 = (bf16[9,112,1024]{2,1,0:T(8,128)(2,1)}, bf16[9,112,1024]{2,1,0:T(8,128)(2,1)S(1)}, u32[]{:S(2)}, u32[]{:S(2)}) collective-permute-start(bf16[9,112,1024]{2,1,0:T(8,128)(2,1)} %branch_9_fun.4), channel_id=1, source_target_pairs={{0,4},{1,5},{2,6},{3,7},{4,0},{5,1},{6,2},{7,3},{8,12},{9,13},{10,... | collective-permute-start | bytes 6193160 | tf_op jit(solution)/shard_map/cond/branch_9_fun/ppermute | solution.py:194
  495.5 1.3 copy-start.16
  501.2 4.8 copy-start.49
  501.2 5.0 copy-start.44
  501.2 5.1 copy-start.41
  501.2 5.2 copy-start.46
  501.2 7.5 %copy-start.34 = (bf16[32,16,8]{0,2,1:T(8,128)(2,1)S(1)}, bf16[32,16,8]{0,2,1:T(8,128)(2,1)}, u32[]{:S(2)}) copy-start(bf16[32,16,8]{0,2,1:T(8,128)(2,1)} %copy-done.33) | copy-start | bytes 24580
  501.2 7.5 %copy-start.36 = (bf16[32,16,8]{0,2,1:T(8,128)(2,1)S(1)}, bf16[32,16,8]{0,2,1:T(8,128)(2,1)}, u32[]{:S(2)}) copy-start(bf16[32,16,8]{0,2,1:T(8,128)(2,1)} %copy-done.35) | copy-start | bytes 24580
  501.2 10.9 %copy-start.14 = (bf16[32,8,1024]{2,1,0:T(8,128)(2,1)S(1)}, bf16[32,8,1024]{2,1,0:T(8,128)(2,1)}, u32[]{:S(2)}) copy-start(bf16[32,8,1024]{2,1,0:T(8,128)(2,1)} %all_to_all.25) | copy-start | bytes 1572868
  501.3 51.0 %all-to-all-start.1 = ((bf16[16,112,1024]{2,1,0:T(8,128)(2,1)}), bf16[16,112,1024]{2,1,0:T(8,128)(2,1)}, u32[]{:S(2)}, u32[]{:S(2)}) async-start(bf16[16,112,1024]{2,1,0:T(8,128)(2,1)} %get-tuple-element.390), calls=%async_computation.1 | async-start | bytes 7340032 | tf_op jit(solution)/shard_map/all_to_all | solution.py:347
